TPU v7x, 512 devices: a whole 4x4x16 slice. The times are simulated.
512 devices in a mesh: batch: 128 (over z, x, core), tower: 4 (over y).
Axes of the slice: x: 4, y: 4, z: 16, core: 2. Of those that a mesh axis runs over, the one named last changes fastest.
Arguments:
- images: bfloat16 [65536, 1152], P('batch'), may hold values from -13 to 13
- texts: bfloat16 [65536, 1152], P(('batch', 'tower')), may hold values from -13 to 13
- log_scale: float32 [], replicated, may hold values from 1.5 to 3
- bias: float32 [], replicated, may hold values from -2 to 0.5
- block_mask: int32 [256, 8], P('batch'), may hold values from 0 to 1, as said below
- data_order: int32 [65536], P(('batch', 'tower')), may hold values from 0 to 65535, as said below
Outputs:
- image_grad: float32 [65536, 1152], P(('batch', 'tower'))
- text_grad: float32 [65536, 1152], P(('batch', 'tower'))
- pair_loss: float32 [], replicated
Inputs may be any that keep to these rules, and one draw needn't show every extreme that they name: block_mask[p, c] refers to text block 2 * (p // 2) + c; it is 1 exactly where that block exists and belongs to the same cluster as block p, clusters being runs of consecutive blocks of uneven lengths; so it is 1 for c = p % 2 and 0 for blocks past the last. data_order is a permutation; data_order[i] // 128 % 4 equals i // 128 % 4; the 128 rows of each run i // 128 send exactly 1 row to each batch index b, meaning data_order // 512 == b.
All inputs are finite; a program needn't handle non-finite values.
Results may differ from a plain program's by a relative error of at most 0.00031.
Values may be sent and summed in bfloat16 or wider, within the bound.
A program may use at most 64 MiB of HBM per device.

v0:
```python
import jax
import jax.numpy as jnp
from jax import lax
from jax.sharding import PartitionSpec as P

NORM_EPS = 1e-06


def passed_along(block, axis, distance):
    devices = range(lax.axis_size(axis))
    route = [(i - distance, i) for i in devices if i - distance in devices]
    return lax.ppermute(block, axis, route)


def unit_rows(values):
    wide = values.astype(jnp.float32)
    inv_norm = lax.rsqrt(jnp.sum(wide * wide, axis=-1, keepdims=True) + NORM_EPS)
    return (wide * inv_norm, inv_norm)


def pair_terms(img_unit, candidates, selected, positive, logit_scale, bias):
    logits = (
        logit_scale
        * lax.dot_general(
            img_unit, candidates, (((1,), (1,)), ((), ())), preferred_element_type=jnp.float32
        )
        + bias
    )
    sign_of = 2.0 * positive - 1.0
    loss_part = jnp.sum(selected * jax.nn.softplus(-sign_of * logits))
    coeffs = (selected * logit_scale * (jax.nn.sigmoid(logits) - positive)).astype(jnp.bfloat16)
    return (coeffs, loss_part)


def shards(images, texts, log_scale, bias, block_mask, data_order):
    towers = lax.axis_size("tower")
    tower_at = lax.axis_index("tower")
    rows_group = images.shape[0]
    quarter = texts.shape[0]
    width_d = images.shape[1]
    blk_count = block_mask.shape[0]
    cand_blocks = block_mask.shape[1]
    window = cand_blocks // blk_count
    block_rows = rows_group // blk_count
    logit_scale = jnp.exp(log_scale)
    img_unit32, img_inv = unit_rows(images)
    img_unit = img_unit32.astype(jnp.bfloat16)
    txt_unit32, txt_inv = unit_rows(texts)
    txt_unit = txt_unit32.astype(jnp.bfloat16)
    pieces = [txt_unit]
    for offset in range(1, window):
        pieces.append(passed_along(txt_unit, ("batch", "tower"), -towers * offset))
    candidates = jnp.concatenate(pieces, axis=0)
    local_rows = tower_at * quarter + jnp.arange(quarter, dtype=jnp.int32)
    col_block = (
        jnp.arange(window, dtype=jnp.int32)[:, None] * blk_count
        + (local_rows // block_rows)[None, :]
    ).reshape(-1)
    one_hot = (col_block[:, None] == jnp.arange(cand_blocks, dtype=jnp.int32)[None, :]).astype(
        jnp.float32
    )
    sel_blocks = jnp.dot(block_mask.astype(jnp.float32), one_hot.T)
    selected = jnp.broadcast_to(
        sel_blocks[:, None, :], (blk_count, block_rows, window * quarter)
    ).reshape(rows_group, window * quarter)
    col_target = jnp.concatenate([local_rows, jnp.full(((window - 1) * quarter,), -1, jnp.int32)])
    positive = (jnp.arange(rows_group, dtype=jnp.int32)[:, None] == col_target[None, :]).astype(
        jnp.float32
    )
    coeffs, loss_part = pair_terms(img_unit, candidates, selected, positive, logit_scale, bias)
    txt_terms = lax.dot_general(
        coeffs, img_unit, (((0,), (0,)), ((), ())), preferred_element_type=jnp.float32
    )
    summed_text = txt_terms[:quarter]
    for offset in range(1, window):
        summed_text = summed_text + passed_along(
            txt_terms[offset * quarter : (offset + 1) * quarter],
            ("batch", "tower"),
            towers * offset,
        )
    text_grad = (
        summed_text - txt_unit32 * jnp.sum(txt_unit32 * summed_text, axis=-1, keepdims=True)
    ) * txt_inv
    own_back = lax.psum_scatter(
        jnp.dot(coeffs, candidates, preferred_element_type=jnp.float32),
        "tower",
        scatter_dimension=0,
        tiled=True,
    )
    own_unit = lax.dynamic_slice_in_dim(img_unit32, tower_at * quarter, quarter, 0)
    own_inv = lax.dynamic_slice_in_dim(img_inv, tower_at * quarter, quarter, 0)
    own_grad = (
        own_back - own_unit * jnp.sum(own_unit * own_back, axis=-1, keepdims=True)
    ) * own_inv
    send_order = jnp.argsort(data_order)
    send_rows = own_grad[send_order]
    slot_ids = data_order[send_order] % quarter
    arrived, arrived_slots = (
        lax.all_to_all(send_rows, "batch", split_axis=0, concat_axis=0, tiled=True),
        lax.all_to_all(slot_ids, "batch", split_axis=0, concat_axis=0, tiled=True),
    )
    image_grad = jnp.zeros((quarter, width_d), jnp.float32).at[arrived_slots].set(arrived)
    pair_count = jnp.sum(selected)
    loss_sum, count_sum = lax.psum((loss_part, pair_count), ("batch", "tower"))
    return (image_grad, text_grad, loss_sum / count_sum)


def solution(mesh):
    in_specs = (
        P("batch", None),
        P(("batch", "tower"), None),
        P(),
        P(),
        P("batch", None),
        P(("batch", "tower")),
    )
    out_specs = (P(("batch", "tower"), None), P(("batch", "tower"), None), P())
    return jax.shard_map(shards, mesh=mesh, in_specs=in_specs, out_specs=out_specs, check_vma=False)
```

profile of v0, /device:TPU:1, one launch (start us, length us, event | category | flops | bytes accessed | tf_op | source)
XLA Modules:
  0.0 270.2 jit_solution(10300427098139993436)
XLA Ops:
  7.2 0.0 copy-start.1
  7.2 0.0 reduce-scatter.2.cloned.1.call-start
  7.2 1.2 fusion.11
  8.4 1.1 fusion.7
  9.5 1.3 collective-permute-start.2
  10.8 1.3 collective-permute-start.1
  12.1 8.8 %collective-permute-start = (bf16[128,1152]{1,0:T(8,128)(2,1)S(1)}, bf16[128,1152]{1,0:T(8,128)(2,1)S(1)}, u32[]{:S(2)}, u32[]{:S(2)}) collective-permute-start(bf16[128,1152]{1,0:T(8,128)(2,1)S(1)} %fusion.7), channel_id=1, source_target_pairs={{4,0},{5,1},{6,2},{7,3},{8,4},{9,5},{10,6},{11,7},{12,8},{13,9},{1... | collective-permute-start | bytes 884744 | tf_op jit(solution)/shard_map/ppermute | solution.py:12
  22.3 1.6 fusion
  23.9 0.1 add_bitcast_fusion
  23.9 0.9 convolution_bitcast_fusion
  24.9 0.0 collective-permute-done.2
  24.9 8.2 %collective-permute-done.1 = bf16[128,1152]{1,0:T(8,128)(2,1)S(1)} collective-permute-done((bf16[128,1152]{1,0:T(8,128)(2,1)S(1)}, bf16[128,1152]{1,0:T(8,128)(2,1)S(1)}, u32[]{:S(2)}, u32[]{:S(2)}) %collective-permute-start.1) | collective-permute-done | bytes 294944 | tf_op jit(solution)/shard_map/ppermute | solution.py:12
  33.1 1.0 collective-permute-done
  34.1 0.0 copy-done.1
  34.1 2.6 fusion.4
  36.8 0.8 copy-done.4
  37.5 2.3 fusion.21
  39.8 0.0 reduce-scatter.2.cloned.1.call-update
  39.8 0.6 copy-done
  40.5 2.5 sort.17
  43.0 1.2 gather_fusion
  44.3 0.7 copy.11
  45.0 18.3 %all-to-all-start = ((s32[128,1,1]{2,1,0:T(1,128)}), s32[128,1,1]{2,1,0:T(1,128)}, u32[]{:S(2)}, u32[]{:S(2)}) async-start(s32[128,1,1]{2,1,0:T(1,128)} %copy.11), calls=%async_computation | async-start | bytes 131072 | tf_op jit(solution)/shard_map/all_to_all | solution.py:100
  63.3 0.6 dynamic-slice.3
  63.9 0.2 convert_multiply_fusion
  64.1 18.3 %reduce-scatter.2.cloned.1.call-done = f32[128,1152]{1,0:T(8,128)} async-done(((f32[512,1152]{1,0:T(8,128)}), f32[128,1152]{1,0:T(8,128)}) %reduce-scatter.2.cloned.1.call-update) | async-done | bytes 589840 | tf_op jit(solution)/shard_map/reduce_scatter | solution.py:84
  82.4 1.2 multiply_reduce_fusion
  83.6 1.4 subtract_multiply_fusion
  85.0 0.9 gather_fusion.1
  85.9 1.4 copy.12
  87.3 0.0 all-to-all-done
  87.3 17.0 %all-to-all-start.1 = ((f32[128,1,1152]{2,1,0:T(1,128)}), f32[128,1,1152]{2,1,0:T(1,128)}, u32[]{:S(2)}, u32[]{:S(2)}) async-start(f32[128,1,1152]{2,1,0:T(1,128)} %copy.12), calls=%async_computation.2 | async-start | bytes 1179648 | tf_op jit(solution)/shard_map/all_to_all | solution.py:99
  104.3 2.0 fusion.17
  106.3 0.0 copy-start.3
  106.3 1.1 fusion.29
  107.4 5.9 %collective-permute-start.5 = (f32[128,1152]{1,0:T(8,128)}, f32[128,1152]{1,0:T(8,128)}, u32[]{:S(2)}, u32[]{:S(2)}) collective-permute-start(f32[128,1152]{1,0:T(8,128)} %get-tuple-element.10), channel_id=1, source_target_pairs={{0,12},{1,13},{2,14},{3,15},{4,16},{5,17},{6,18},{7,19},{8,20},{9,... | collective-permute-start | bytes 1769480 | tf_op jit(solution)/shard_map/ppermute | solution.py:12
  113.3 2.2 collective-permute-start.4
  115.5 2.1 collective-permute-start.3
  117.6 0.9 broadcast_reduce_fusion
  118.4 3.2 %reduce.1 = s32[128]{0:T(128)S(1)} reduce(s32[128,1,1]{2,1,0:T(1,128)} %all-to-all-done, s32[]{:T(128)} %constant.24.clone.1), dimensions={1,2}, to_apply=%all_to_all.14.reduce_sub_computation | reduce | bytes 1028 | tf_op jit(solution)/shard_map/all_to_all | solution.py:100
  121.6 134.2 %all-reduce.1 = (f32[]{:T(128)}, f32[]{:T(128)}) all-reduce(f32[]{:T(128)} %get-tuple-element.12, f32[]{:T(128)} %broadcast_reduce_fusion), channel_id=1, replica_groups=mesh['batch'=128,'tower'=4] {'batch','tower'}, use_global_device_ids=true, to_apply=%region_8.9 | all-reduce | flops 2 | bytes 16 | tf_op jit(solution)/shard_map/psum | solution.py:104
  257.1 0.0 collective-permute-done.5
  257.1 0.0 collective-permute-done.4
  257.1 0.0 collective-permute-done.3
  257.2 1.7 fusion.8
  258.8 1.0 fusion.10
  259.9 0.0 all-to-all-done.1
  259.9 2.4 scatter_custom_fusion
  (16 shorter events, 0.1 us)
Async XLA Ops:
  7.2 27.0 %copy-start.1 = (bf16[512,1152]{1,0:T(8,128)(2,1)S(1)}, bf16[512,1152]{1,0:T(8,128)(2,1)}, u32[]{:S(2)}) copy-start(bf16[512,1152]{1,0:T(8,128)(2,1)} %param.6) | copy-start | bytes 3538948
  7.2 75.2 %reduce-scatter.2.cloned.1.call-start = ((), (), s32[]{:S(2)}) async-start(), calls=%async_computation.3 | async-start | bytes 2949120 | tf_op jit(solution)/shard_map/reduce_scatter | solution.py:84
  9.5 15.4 %collective-permute-start.2 = (bf16[128,1152]{1,0:T(8,128)(2,1)S(1)}, bf16[128,1152]{1,0:T(8,128)(2,1)S(1)}, u32[]{:S(2)}, u32[]{:S(2)}) collective-permute-start(bf16[128,1152]{1,0:T(8,128)(2,1)S(1)} %fusion.7), channel_id=1, source_target_pairs={{12,0},{13,1},{14,2},{15,3},{16,4},{17,5},{18,6},{19,7},{20,8},{21... | collective-permute-start | bytes 884744 | tf_op jit(solution)/shard_map/ppermute | solution.py:12
  10.8 22.3 %collective-permute-start.1 = (bf16[128,1152]{1,0:T(8,128)(2,1)S(1)}, bf16[128,1152]{1,0:T(8,128)(2,1)S(1)}, u32[]{:S(2)}, u32[]{:S(2)}) collective-permute-start(bf16[128,1152]{1,0:T(8,128)(2,1)S(1)} %fusion.7), channel_id=1, source_target_pairs={{8,0},{9,1},{10,2},{11,3},{12,4},{13,5},{14,6},{15,7},{16,8},{17,9... | collective-permute-start | bytes 884744 | tf_op jit(solution)/shard_map/ppermute | solution.py:12
  12.1 22.0 %collective-permute-start = (bf16[128,1152]{1,0:T(8,128)(2,1)S(1)}, bf16[128,1152]{1,0:T(8,128)(2,1)S(1)}, u32[]{:S(2)}, u32[]{:S(2)}) collective-permute-start(bf16[128,1152]{1,0:T(8,128)(2,1)S(1)} %fusion.7), channel_id=1, source_target_pairs={{4,0},{5,1},{6,2},{7,3},{8,4},{9,5},{10,6},{11,7},{12,8},{13,9},{1... | collective-permute-start | bytes 884744 | tf_op jit(solution)/shard_map/ppermute | solution.py:12
  36.7 0.8 copy-start.4
  39.8 0.7 copy-start
  45.0 42.3 %all-to-all-start = ((s32[128,1,1]{2,1,0:T(1,128)}), s32[128,1,1]{2,1,0:T(1,128)}, u32[]{:S(2)}, u32[]{:S(2)}) async-start(s32[128,1,1]{2,1,0:T(1,128)} %copy.11), calls=%async_computation | async-start | bytes 131072 | tf_op jit(solution)/shard_map/all_to_all | solution.py:100
  64.1 18.3 %copy-start.2 = (f32[512,1152]{1,0:T(8,128)}, f32[512,1152]{1,0:T(8,128)S(1)}, u32[]{:S(2)}) copy-start(f32[512,1152]{1,0:T(8,128)S(1)} %convert_multiply_fusion) | copy-start | bytes 7077892
  87.3 172.6 %all-to-all-start.1 = ((f32[128,1,1152]{2,1,0:T(1,128)}), f32[128,1,1152]{2,1,0:T(1,128)}, u32[]{:S(2)}, u32[]{:S(2)}) async-start(f32[128,1,1152]{2,1,0:T(1,128)} %copy.12), calls=%async_computation.2 | async-start | bytes 1179648 | tf_op jit(solution)/shard_map/all_to_all | solution.py:99
  106.3 150.9 %copy-start.3 = (bf16[128,1152]{1,0:T(8,128)(2,1)S(1)}, bf16[128,1152]{1,0:T(8,128)(2,1)}, u32[]{:S(2)}) copy-start(bf16[128,1152]{1,0:T(8,128)(2,1)} %param.7) | copy-start | bytes 884740
  107.4 149.7 %collective-permute-start.5 = (f32[128,1152]{1,0:T(8,128)}, f32[128,1152]{1,0:T(8,128)}, u32[]{:S(2)}, u32[]{:S(2)}) collective-permute-start(f32[128,1152]{1,0:T(8,128)} %get-tuple-element.10), channel_id=1, source_target_pairs={{0,12},{1,13},{2,14},{3,15},{4,16},{5,17},{6,18},{7,19},{8,20},{9,... | collective-permute-start | bytes 1769480 | tf_op jit(solution)/shard_map/ppermute | solution.py:12
  113.3 143.9 %collective-permute-start.4 = (f32[128,1152]{1,0:T(8,128)}, f32[128,1152]{1,0:T(8,128)}, u32[]{:S(2)}, u32[]{:S(2)}) collective-permute-start(f32[128,1152]{1,0:T(8,128)} %get-tuple-element.11), channel_id=1, source_target_pairs={{0,8},{1,9},{2,10},{3,11},{4,12},{5,13},{6,14},{7,15},{8,16},{9,17... | collective-permute-start | bytes 1769480 | tf_op jit(solution)/shard_map/ppermute | solution.py:12
  115.5 141.7 %collective-permute-start.3 = (f32[128,1152]{1,0:T(8,128)S(1)}, f32[128,1152]{1,0:T(8,128)}, u32[]{:S(2)}, u32[]{:S(2)}) collective-permute-start(f32[128,1152]{1,0:T(8,128)S(1)} %get-tuple-element.9), channel_id=1, source_target_pairs={{0,4},{1,5},{2,6},{3,7},{4,8},{5,9},{6,10},{7,11},{8,12},{9,13},{1... | collective-permute-start | bytes 1769480 | tf_op jit(solution)/shard_map/ppermute | solution.py:12
Sparse Core Ops, SparseCore 0:
  39.9 42.3 reduce-scatter.1
where the time goes:
time: 271 us; the launch traced here: 270 us
  blocking collectives  134 us (49%)
  starting transfers between devices  56.9 us (21%)
  waiting for transfers between devices  27.5 us (10%)
  between operations  17.9 us (7%)
  other arithmetic  16.1 us (6%)
  local copies, waits for them, and re-layouts  9.77 us (4%)
  matrix products  7.79 us (3%)
    psum x1, blocking collectives, shards(): loss_sum, count_sum = lax.psum((loss_part, pair_count), ('batch', 'tower'))  134 us
    ppermute x6, starting transfers between devices, passed_along(): return lax.ppermute(block, axis, route)  21.5 us
    all_to_all x1, starting transfers between devices, shards(): lax.all_to_all(slot_ids, 'batch', split_axis=0, concat_axis=0, tiled=True)  18.3 us
    reduce_scatter x1, waiting for transfers between devices, shards(): lax.psum_scatter(jnp.dot(coeffs, candidates, preferred_element_type=jnp.f...  18.3 us
    all_to_all x1, starting transfers between devices, shards(): lax.all_to_all(send_rows, 'batch', split_axis=0, concat_axis=0, tiled=True)  17 us
    ppermute x6, waiting for transfers between devices, passed_along(): return lax.ppermute(block, axis, route)  9.26 us
  transfers between devices with their start and end apart: 9, of which 3 were waited for; matrix products, arithmetic and copies ran while one was open for 8% of the time, Pallas kernels for 0%

commit v1 on v0

v1 whole, which is shorter than its diff:
```python
import functools

import jax
import jax.numpy as jnp
from jax import lax
from jax.experimental import pallas as pl
from jax.experimental.pallas import tpu as pltpu
from jax.sharding import PartitionSpec as P

NORM_EPS = 1e-06
MESH = pl.DeviceIdType.MESH
LANES = 128
TOP = 32760.0
LOG_STEP = 0.6931471805599453 / 256.0
NT = (((1,), (1,)), ((), ()))
TN = (((0,), (0,)), ((), ()))
NN = (((1,), (0,)), ((), ()))


def mxu(a, b, dims):
    return lax.dot_general(a, b, dims, preferred_element_type=jnp.float32)


def row_inv(wide):
    return lax.rsqrt(jnp.sum(wide * wide, axis=-1, keepdims=True) + NORM_EPS)


def as_codes(rows):
    top = jnp.maximum(jnp.max(jnp.abs(rows), axis=-1, keepdims=True), 1e-30)
    power = jnp.ceil(jnp.log(top) * (1.0 / LOG_STEP))
    codes = jnp.round(rows * (TOP * jnp.exp(power * -LOG_STEP))).astype(jnp.int32)
    return codes, power.astype(jnp.int32)


def step_of(power):
    return jnp.exp(power.astype(jnp.float32) * LOG_STEP) * (1.0 / TOP)


def lane_ids(rows):
    return lax.broadcasted_iota(jnp.int32, (rows, LANES), 1)


def words_of(codes, extras):
    low = [codes[:, LANES * (k + 4) : LANES * (k + 5)] for k in range(4)] + [extras]
    order = (0, 1, 2, 3, 8)
    return [
        (codes[:, LANES * k : LANES * (k + 1)] << 16) | (other & 0xFFFF)
        for k, other in zip(order, low, strict=True)
    ]


def high_of(word):
    return word >> 16


def low_of(word):
    return (word << 16) >> 16


def columns_of(words, high, low):
    return [high(words[k]) for k in range(4)] + [low(words[k]) for k in range(4)] + [high(words[4])]


def rows_from(ref):
    words = [ref[:, LANES * k : LANES * (k + 1)] for k in range(5)]
    extras = low_of(words[4])
    codes = jnp.concatenate(columns_of(words, high_of, low_of), axis=1)
    return codes.astype(jnp.float32) * step_of(extras[:, 0:1]), extras


def loss_fields(total):
    power = jnp.ceil(jnp.log(jnp.maximum(total, 1e-30)) * (1.0 / 0.6931471805599453))
    scaled = total * jnp.exp(power * -0.6931471805599453) * 8192.0
    first = jnp.floor(scaled)
    second = jnp.floor((scaled - first) * 16384.0)
    return [v.astype(jnp.int32) for v in (power, first, second)]


def loss_from(power, first, second):
    wide = first.astype(jnp.float32) + second.astype(jnp.float32) * (1.0 / 16384.0)
    return wide * jnp.exp(power.astype(jnp.float32) * 0.6931471805599453) * (1.0 / 8192.0)


def kernel(
    images_ref,
    texts_ref,
    log_scale_ref,
    bias_ref,
    mask_ref,
    order_ref,
    image_grad_ref,
    text_grad_ref,
    loss_ref,
    img_unit,
    img_inv,
    cand,
    coeffs,
    loss_acc,
    own_text,
    own_image,
    part_send,
    part_recv,
    tower_send,
    tower_recv,
    row_send,
    row_recv,
    cand_sent,
    cand_here,
    part_sent,
    part_here,
    tower_sent,
    tower_here,
    row_sent,
    row_here,
    row_own,
):
    n_batch = lax.axis_size("batch")
    n_tower = lax.axis_size("tower")
    me = lax.axis_index("batch")
    tower = lax.axis_index("tower")
    core = lax.rem(me, 2)
    quarter, width = texts_ref.shape

    def batch_at(offset):
        return lax.rem(me + (n_batch + offset), n_batch)

    def tower_at(offset):
        return lax.rem(tower + offset, n_tower)

    barrier = pltpu.get_barrier_semaphore()

    def greet(i, _):
        pl.semaphore_signal(
            barrier, 1, device_id={"batch": lax.rem(me + i, n_batch)}, device_id_type=MESH
        )
        return 0

    lax.fori_loop(1, n_batch, greet, 0)
    for d in range(1, n_tower):
        pl.semaphore_signal(barrier, 1, device_id={"tower": tower_at(d)}, device_id_type=MESH)

    wide = texts_ref[...].astype(jnp.float32)
    txt_inv = row_inv(wide)
    cand[0] = (wide * txt_inv).astype(jnp.bfloat16)

    pl.semaphore_wait(barrier, n_batch - 1 + n_tower - 1)

    def cand_copy(source, target, dest, sem):
        return pltpu.make_async_remote_copy(
            src_ref=cand.at[source],
            dst_ref=cand.at[target],
            send_sem=cand_sent.at[sem],
            recv_sem=cand_here.at[target],
            device_id={"batch": dest},
            device_id_type=MESH,
        )

    first_slot = 3 - 2 * core
    sibling = me + 1 - 2 * core
    outward = cand_copy(0, 1 + 2 * core, batch_at(-1 - 2 * core), 0)
    outward.start()

    @pl.when(core == 1)
    def _():
        cand_copy(0, 1, sibling, 1).start()

    def norm(q, _):
        rows = pl.ds(q * quarter, quarter)
        values = images_ref[rows, :].astype(jnp.float32)
        inv = row_inv(values)
        img_inv[rows, :] = inv
        img_unit[rows, :] = (values * inv).astype(jnp.bfloat16)
        return 0

    lax.fori_loop(0, n_tower, norm, 0)

    logit_scale = jnp.exp(jnp.full((1, LANES), log_scale_ref[0], jnp.float32))
    bias = bias_ref[0]
    loss_acc[...] = jnp.zeros_like(loss_acc)
    diagonal = lax.broadcasted_iota(jnp.int32, (quarter, quarter), 0) == lax.broadcasted_iota(
        jnp.int32, (quarter, quarter), 1
    )

    def pairs(k, own):
        block = cand[k]

        def some(q, _):
            rows = pl.ds(pl.multiple_of(q * quarter, quarter), quarter)
            logits = logit_scale * mxu(img_unit[rows, :], block, NT) + bias
            small = jnp.exp(-jnp.abs(logits))
            share = 1.0 / (1.0 + small)
            sigmoid = jnp.where(logits >= 0.0, share, small * share)
            loss = jnp.maximum(logits, 0.0) + jnp.log1p(small)
            chosen = mask_ref[q // 2, 2 * k + tower // 2].astype(jnp.float32)
            if own:
                positive = jnp.where(diagonal & (q == tower), 1.0, 0.0)
                loss = loss - positive * logits
                sigmoid = sigmoid - positive
            loss_acc[...] += chosen * loss
            cols = pl.ds(pl.multiple_of(k * quarter, quarter), quarter)
            coeffs[rows, cols] = (chosen * logit_scale * sigmoid).astype(jnp.bfloat16)
            return 0

        lax.fori_loop(0, n_tower, some, 0)

    def text_part(k):
        cols = pl.ds(pl.multiple_of(k * quarter, quarter), quarter)
        return mxu(coeffs[:, cols], img_unit[...], TN)

    def put_words(ref, slot, codes, extras):
        for j, word in enumerate(words_of(codes, extras)):
            ref[slot, :, LANES * j : LANES * (j + 1)] = word

    def part_copy(k):
        return pltpu.make_async_remote_copy(
            src_ref=part_send.at[k - 1],
            dst_ref=part_recv.at[k - 1],
            send_sem=part_sent.at[k - 1],
            recv_sem=part_here.at[k - 1],
            device_id={"batch": batch_at(k)},
            device_id_type=MESH,
        )

    def text_part_out(k):
        codes, power = as_codes(text_part(k))
        put_words(part_send, k - 1, codes, jnp.where(lane_ids(quarter) == 0, power, 0))
        part_copy(k).start()

    pairs(0, True)
    own_text[...] = text_part(0)

    cand_copy(0, first_slot, me, 0).wait_recv()
    cand_copy(first_slot, 2, sibling, 2).start()

    @pl.when(core == 1)
    def _():
        cand_copy(1, 3, batch_at(-2), 3).start()

    pairs(first_slot, False)
    text_part_out(first_slot)
    second_slot = 1 + core
    cand_copy(0, second_slot, me, 0).wait_recv()
    pairs(second_slot, False)
    text_part_out(second_slot)
    third_slot = 2 + core
    cand_copy(0, third_slot, me, 0).wait_recv()
    pairs(third_slot, False)

    total = jnp.sum(jnp.sum(loss_acc[...], axis=1, keepdims=True), axis=0, keepdims=True)

    def image_part(q):
        rows = pl.ds(pl.multiple_of(q * quarter, quarter), quarter)
        back = mxu(coeffs[rows, :], cand[...].reshape(4 * quarter, width), NN)
        inv = img_inv[rows, :]
        unit = images_ref[rows, :].astype(jnp.float32) * inv
        return (back - unit * jnp.sum(unit * back, axis=-1, keepdims=True)) * inv

    def fields(head, rest):
        lane = lane_ids(quarter)
        out = jnp.where(lane == 0, head, 0)
        for j, value in enumerate(rest):
            out = jnp.where(lane == j + 1, value, out)
        return out

    def tower_copy(d):
        return pltpu.make_async_remote_copy(
            src_ref=tower_send.at[d - 1],
            dst_ref=tower_recv.at[d - 1],
            send_sem=tower_sent.at[d - 1],
            recv_sem=tower_here.at[d - 1],
            device_id={"tower": tower_at(d)},
            device_id_type=MESH,
        )

    loss_parts = loss_fields(total)
    for d in (2, 1, 3):
        codes, power = as_codes(image_part(tower_at(d)))
        put_words(tower_send, d - 1, codes, fields(power, loss_parts))
        tower_copy(d).start()

    text_part_out(third_slot)
    own_image[...] = image_part(tower)

    grad = own_image[...]
    for d in (1, 3, 2):
        tower_copy(d).wait_recv()
        rows, extras = rows_from(tower_recv.at[d - 1])
        grad = grad + rows
        total = total + loss_from(extras[0:1, 1:2], extras[0:1, 2:3], extras[0:1, 3:4])
    codes, power = as_codes(grad)
    order = order_ref[...]
    picks = lax.broadcasted_iota(jnp.int32, (quarter, quarter), 0) == order // (n_tower * quarter)
    slots = jnp.sum(jnp.where(picks, lax.rem(order, quarter), 0), axis=1, keepdims=True)
    one_hot = jnp.where(picks, 1.0, 0.0).astype(jnp.bfloat16)

    def bytes_of(whole):
        return whole.astype(jnp.float32).astype(jnp.bfloat16)

    def moved(matrix, high, low, dims):
        return mxu(matrix, bytes_of(high), dims) * 256.0 + mxu(matrix, bytes_of(low), dims)

    def moved_whole(whole):
        return moved(one_hot, whole >> 8, whole & 0xFF, NN).astype(jnp.int32)

    count = mask_ref[0, 0] * 0
    for p in range(mask_ref.shape[0]):
        for c in range(mask_ref.shape[1]):
            count = count + mask_ref[p, c]
    sent_power = moved_whole(jnp.where(lane_ids(quarter) == 0, power, 0))
    extras = sent_power
    for j, value in enumerate([slots, count, *loss_fields(total)]):
        extras = jnp.where(lane_ids(quarter) == j + 1, value, extras)
    for j, word in enumerate(words_of(moved_whole(codes), extras)):
        for g in range(quarter // 8):
            row_send[pl.ds(40 * g + j, 8, stride=5), :] = word[8 * g : 8 * (g + 1), :]

    def row_copy(dest):
        return pltpu.make_async_remote_copy(
            src_ref=row_send.at[pl.ds(dest * 5, 5)],
            dst_ref=row_recv.at[pl.ds(me * 5, 5)],
            send_sem=row_sent,
            recv_sem=row_here,
            device_id={"batch": dest},
            device_id_type=MESH,
        )

    def send_row(i, _):
        half = (i + 1) // 2
        offset = n_batch // 2 + half * (1 - 2 * lax.rem(i, 2))
        row_copy(lax.rem(me + offset, n_batch)).start()
        return 0

    lax.fori_loop(0, n_batch - 1, send_row, 0)
    here = pl.ds(me * 5, 5)
    own_copy = pltpu.make_async_copy(row_send.at[here], row_recv.at[here], row_own)
    own_copy.start()

    back = own_text[...]
    for k in (1, 2, 3):
        part_copy(k).wait_recv()
        rows, _ = rows_from(part_recv.at[k - 1])
        back = back + rows
    wide = texts_ref[...].astype(jnp.float32)
    inv = row_inv(wide)
    unit = wide * inv
    text_grad_ref[...] = (back - unit * jnp.sum(unit * back, axis=-1, keepdims=True)) * inv

    own_copy.wait()
    all_rows = row_recv.at[pl.ds(0, (n_batch - 1) * 5)]
    pltpu.make_async_copy(all_rows, all_rows, row_here).wait()
    words = [
        jnp.concatenate(
            [row_recv[pl.ds(40 * g + j, 8, stride=5), :] for g in range(quarter // 8)], axis=0
        )
        for j in range(5)
    ]
    extras = low_of(words[4])
    places = jnp.where(lane_ids(quarter) == extras[:, 1:2], 1.0, 0.0).astype(jnp.bfloat16)
    steps = moved(places, extras >> 8, extras & 0xFF, TN)[:, 0:1]
    steps = jnp.exp(steps * LOG_STEP) * (1.0 / TOP)
    parts = columns_of(words, high_of, low_of)
    for j, whole in enumerate(parts):
        image_grad_ref[:, LANES * j : LANES * (j + 1)] = (
            moved(places, whole >> 8, whole & 0xFF, TN) * steps
        )
    losses = loss_from(extras[:, 3:4], extras[:, 4:5], extras[:, 5:6])
    counts = extras[:, 2:3].astype(jnp.float32) * float(4 * quarter * quarter)
    loss_ref[...] = jnp.sum(losses, axis=0, keepdims=True) / jnp.sum(
        counts, axis=0, keepdims=True
    )

    outward.wait_send()
    cand_copy(first_slot, 2, sibling, 2).wait_send()

    @pl.when(core == 1)
    def _():
        cand_copy(0, 1, sibling, 1).wait_send()
        cand_copy(1, 3, batch_at(-2), 3).wait_send()

    for k in (1, 2, 3):
        part_copy(k).wait_send()
        tower_copy(k).wait_send()
    all_sent = row_send.at[pl.ds(0, (n_batch - 1) * 5)]
    pltpu.make_async_copy(all_sent, all_sent, row_sent).wait()


def shards(images, texts, log_scale, bias, block_mask, data_order):
    rows_group, width = images.shape
    quarter = texts.shape[0]
    words = 5 * LANES
    vmem = pl.BlockSpec(memory_space=pltpu.VMEM)
    smem = pl.BlockSpec(memory_space=pltpu.SMEM)
    dma = pltpu.SemaphoreType.DMA
    image_grad, text_grad, pair_loss = pl.pallas_call(
        kernel,
        out_shape=(
            jax.ShapeDtypeStruct((quarter, width), jnp.float32),
            jax.ShapeDtypeStruct((quarter, width), jnp.float32),
            jax.ShapeDtypeStruct((1, 1), jnp.float32),
        ),
        in_specs=[vmem, vmem, smem, smem, smem, vmem],
        out_specs=(vmem, vmem, vmem),
        scratch_shapes=[
            pltpu.VMEM((rows_group, width), jnp.bfloat16),
            pltpu.VMEM((rows_group, 1), jnp.float32),
            pltpu.VMEM((4, quarter, width), jnp.bfloat16),
            pltpu.VMEM((rows_group, 4 * quarter), jnp.bfloat16),
            pltpu.VMEM((quarter, quarter), jnp.float32),
            pltpu.VMEM((quarter, width), jnp.float32),
            pltpu.VMEM((quarter, width), jnp.float32),
            pltpu.VMEM((3, quarter, words), jnp.int32),
            pltpu.VMEM((3, quarter, words), jnp.int32),
            pltpu.VMEM((3, quarter, words), jnp.int32),
            pltpu.VMEM((3, quarter, words), jnp.int32),
            pltpu.VMEM((quarter * 5, LANES), jnp.int32),
            pltpu.VMEM((quarter * 5, LANES), jnp.int32),
            dma((4,)),
            dma((4,)),
            dma((3,)),
            dma((3,)),
            dma((3,)),
            dma((3,)),
            dma,
            dma,
            dma,
        ],
        compiler_params=pltpu.CompilerParams(
            collective_id=0, has_side_effects=True, vmem_limit_bytes=48 * 1024 * 1024
        ),
    )(
        images,
        texts,
        log_scale.reshape(1),
        bias.reshape(1),
        block_mask,
        data_order.reshape(1, quarter),
    )
    return image_grad, text_grad, pair_loss.reshape(())


def solution(mesh):
    in_specs = (
        P("batch", None),
        P(("batch", "tower"), None),
        P(),
        P(),
        P("batch", None),
        P(("batch", "tower")),
    )
    out_specs = (P(("batch", "tower"), None), P(("batch", "tower"), None), P())
    return jax.shard_map(shards, mesh=mesh, in_specs=in_specs, out_specs=out_specs, check_vma=False)
```

time: 271 us -> 80.6 us (0.30)
  blocking collectives: 134 us -> 0 us
  Pallas kernels: 0 us -> 71.5 us
  starting transfers between devices: 56.9 us -> 0 us
  waiting for transfers between devices: 27.5 us -> 0 us
  other arithmetic: 16.1 us -> 0 us
  between operations: 17.9 us -> 3.69 us
  matrix products: 7.79 us -> 0 us
  local copies, waits for them, and re-layouts: 9.77 us -> 5.19 us
    psum x1 -> x0, blocking collectives: 134 us -> none  [shards(): loss_sum, count_sum = lax.psum((loss_part, pair_count), ('batch', 'tower'))]
    pallas_call x0 -> x1, Pallas kernels: none -> 71.5 us  [shards(): pl.pallas_call(kernel, out_shape=(jax.ShapeDtypeStruct((quarter, width),...]
    all_to_all x2 -> x0, starting transfers between devices: 35.3 us -> none  [the longest x1 18.3 us: shards(): lax.all_to_all(slot_ids, 'batch', split_axis=0, concat_axis=0, tiled=True)]
    ppermute x6 -> x0, starting transfers between devices: 21.5 us -> none  [passed_along(): return lax.ppermute(block, axis, route)]
    reduce_scatter x1 -> x0, waiting for transfers between devices: 18.3 us -> none  [shards(): lax.psum_scatter(jnp.dot(coeffs, candidates, preferred_element_type=jnp.f...]
    ppermute x6 -> x0, waiting for transfers between devices: 9.26 us -> none  [passed_along(): return lax.ppermute(block, axis, route)]
    dot_general x4 -> x0, matrix products: 7.79 us -> none  [the longest x1 2.62 us: pair_terms(): lax.dot_general(img_unit, candidates, (((1,), (1,)), ((), ())), preferred...]
    reduce_sum x5 -> x0, other arithmetic: 6.51 us -> none  [the longest x2 2.77 us: unit_rows(): jnp.sum(wide * wide, axis=-1, keepdims=True) + NORM_EPS]
  transfers between devices with their start and end apart: 9 -> 0, of which waited for: 3 -> 0; matrix products, arithmetic and copies ran while one was open for 8% -> 0% of each run, Pallas kernels for 0% -> 0%
where the time goes in v1:
time: 80.6 us; the launch traced here: 80.3 us
  Pallas kernels  71.5 us (89%)
  local copies, waits for them, and re-layouts  5.19 us (6%)
  between operations  3.69 us (5%)
    pallas_call x1, Pallas kernels, shards(): pl.pallas_call(kernel, out_shape=(jax.ShapeDtypeStruct((quarter, width),...  71.5 us
    unnamed x10, local copies, waits for them, and re-layouts  5.19 us

profile of v1, /device:TPU:1, one launch (start us, length us, event | category | flops | bytes accessed | tf_op | source)
XLA Modules:
  0.0 80.3 jit_solution(9015987351863935239)
XLA Ops:
  1.9 0.0 copy-start
  1.9 1.3 %copy-done = bf16[512,1152]{1,0:T(8,128)(2,1)S(1)} copy-done((bf16[512,1152]{1,0:T(8,128)(2,1)S(1)}, bf16[512,1152]{1,0:T(8,128)(2,1)}, u32[]{:S(2)}) %copy-start) | copy-done | bytes 1179672
  3.2 0.0 copy-start.1
  3.2 1.0 %copy-done.1 = bf16[128,1152]{1,0:T(8,128)(2,1)S(1)} copy-done((bf16[128,1152]{1,0:T(8,128)(2,1)S(1)}, bf16[128,1152]{1,0:T(8,128)(2,1)}, u32[]{:S(2)}) %copy-start.1) | copy-done | bytes 294936
  4.2 0.0 copy-start.2
  4.2 0.7 copy-done.2
  4.8 0.0 copy-start.3
  4.8 0.7 copy-done.3
  5.5 71.5 %shard_map.85 = (f32[128,1152]{1,0:T(8,128)S(1)}, f32[128,1152]{1,0:T(8,128)S(1)}, f32[1,1]{1,0:T(1,128)}) custom-call(bf16[512,1152]{1,0:T(8,128)(2,1)S(1)} %copy-done, bf16[128,1152]{1,0:T(8,128)(2,1)S(1)} %copy-done.1, f32[1]{0:T(128)} %bitcast.4.log_scale_ref, f32[1]{0:T(128)} %bitcast.5.bias_ref, s32[2,8]{1,0:T(2,128)S(1)} %copy-done.2, ...), custom_call_target="tpu_custom_call" | custom-call | tf_op jit(solution)/shard_map/pallas_call | solution.py:394
  77.0 0.8 %copy.14 = f32[128,1152]{1,0:T(8,128)} copy(f32[128,1152]{1,0:T(8,128)S(1)} %get-tuple-element.12) | data formatting | bytes 1179648
  77.8 0.8 %copy.15 = f32[128,1152]{1,0:T(8,128)} copy(f32[128,1152]{1,0:T(8,128)S(1)} %get-tuple-element.13) | data formatting | bytes 1179648
Async XLA Ops:
  1.9 1.3 %copy-start = (bf16[512,1152]{1,0:T(8,128)(2,1)S(1)}, bf16[512,1152]{1,0:T(8,128)(2,1)}, u32[]{:S(2)}) copy-start(bf16[512,1152]{1,0:T(8,128)(2,1)} %images_ref.1) | copy-start | bytes 3538948
  3.2 1.0 %copy-start.1 = (bf16[128,1152]{1,0:T(8,128)(2,1)S(1)}, bf16[128,1152]{1,0:T(8,128)(2,1)}, u32[]{:S(2)}) copy-start(bf16[128,1152]{1,0:T(8,128)(2,1)} %texts_ref.1) | copy-start | bytes 884740
  4.2 0.7 copy-start.2
  4.8 0.7 copy-start.3

commit v2 on v1

v2 whole, which is shorter than its diff:
```python
import functools

import jax
import jax.numpy as jnp
from jax import lax
from jax.experimental import pallas as pl
from jax.experimental.pallas import tpu as pltpu
from jax.sharding import PartitionSpec as P

NORM_EPS = 1e-06
MESH = pl.DeviceIdType.MESH
LANES = 128
TOP = 32760.0
LOG_STEP = 0.6931471805599453 / 256.0
NT = (((1,), (1,)), ((), ()))
TN = (((0,), (0,)), ((), ()))
NN = (((1,), (0,)), ((), ()))


def mxu(a, b, dims):
    return lax.dot_general(a, b, dims, preferred_element_type=jnp.float32)


def row_inv(wide):
    return lax.rsqrt(jnp.sum(wide * wide, axis=-1, keepdims=True) + NORM_EPS)


def as_codes(rows):
    top = jnp.maximum(jnp.max(jnp.abs(rows), axis=-1, keepdims=True), 1e-30)
    power = jnp.ceil(jnp.log(top) * (1.0 / LOG_STEP))
    codes = jnp.round(rows * (TOP * jnp.exp(power * -LOG_STEP))).astype(jnp.int32)
    return codes, power.astype(jnp.int32)


def step_of(power):
    return jnp.exp(power.astype(jnp.float32) * LOG_STEP) * (1.0 / TOP)


def lane_ids(rows):
    return lax.broadcasted_iota(jnp.int32, (rows, LANES), 1)


def words_of(codes, extras):
    group = [codes[:, LANES * k : LANES * (k + 1)] for k in range(9)]
    pairs = [(group[8], extras)] + [(group[k], group[k + 4]) for k in range(4)]
    return [word_of(high, low) for high, low in pairs]


def word_of(high, low):
    return (high << 16) | (low & 0xFFFF)


def high_of(word):
    return word >> 16


def low_of(word):
    return (word << 16) >> 16


def loss_fields(total):
    power = jnp.ceil(jnp.log(jnp.maximum(total, 1e-30)) * (1.0 / 0.6931471805599453))
    scaled = total * jnp.exp(power * -0.6931471805599453) * 8192.0
    first = jnp.floor(scaled)
    second = jnp.floor((scaled - first) * 16384.0)
    return [v.astype(jnp.int32) for v in (power, first, second)]


def loss_from(power, first, second):
    wide = first.astype(jnp.float32) + second.astype(jnp.float32) * (1.0 / 16384.0)
    return wide * jnp.exp(power.astype(jnp.float32) * 0.6931471805599453) * (1.0 / 8192.0)


PLANE = 8
SUM_PARTS = ((0, 2), (2, 3), (3, 4), (4, 5))
ROW_PARTS = ((0, 1), (1, 2), (2, 3), (3, 5))


def kernel(
    images_hbm,
    texts_hbm,
    log_scale_ref,
    bias_ref,
    mask_ref,
    order_hbm,
    image_grad_ref,
    text_grad_ref,
    loss_ref,
    images_ref,
    texts_ref,
    order_ref,
    img_unit,
    img_inv,
    cand,
    coeffs,
    dots,
    loss_acc,
    own_text,
    own_image,
    core_send,
    core_recv,
    part_send,
    part_recv,
    tower_send,
    tower_recv,
    tower_relay,
    row_send,
    row_mid,
    row_recv,
    in_here,
    cand_sent,
    cand_here,
    core_sent,
    core_here,
    part_sent,
    part_here,
    hop_sent,
    hop_here,
    near_sent,
    near_here,
    far_sent,
    far_here,
    plane_sent,
    plane_here,
    row_sent,
    row_here,
    row_own,
):
    n_batch = lax.axis_size("batch")
    n_tower = lax.axis_size("tower")
    n_z = n_batch // PLANE
    me = lax.axis_index("batch")
    tower = lax.axis_index("tower")
    z = me // PLANE
    j = lax.rem(me, PLANE)
    core = lax.rem(me, 2)
    sibling = me + 1 - 2 * core
    quarter, width = texts_ref.shape
    half = quarter // 2

    def batch_at(offset):
        return lax.rem(me + (n_batch + offset), n_batch)

    def tower_at(offset):
        return lax.rem(tower + offset, n_tower)

    def z_step(i):
        return n_z // 2 + ((i + 1) // 2) * (1 - 2 * lax.rem(i, 2))

    def column_at(i):
        return lax.rem(z + z_step(i), n_z) * PLANE + j

    def remote(source, target, sent, here, dest):
        return pltpu.make_async_remote_copy(
            src_ref=source,
            dst_ref=target,
            send_sem=sent,
            recv_sem=here,
            device_id=dest,
            device_id_type=MESH,
        )

    loads = [
        pltpu.make_async_copy(texts_hbm, texts_ref, in_here.at[0]),
        pltpu.make_async_copy(images_hbm, images_ref, in_here.at[1]),
        pltpu.make_async_copy(order_hbm, order_ref, in_here.at[2]),
    ]
    for load in loads:
        load.start()

    chips = n_batch // 2
    relay_to = z * PLANE + lax.rem(j + 2, PLANE)
    relayed = lax.rem(z * (PLANE // 2) + lax.rem(j // 2 + 3, PLANE // 2) + chips - 2, chips) * 2 + 1
    chip_after = lax.rem(me // 2 + 2, chips)
    relay_from = ((chip_after // 4) * 4 + lax.rem(lax.rem(chip_after, 4) + 1, 4)) * 2

    barrier = pltpu.get_barrier_semaphore()

    def greet(dest):
        pl.semaphore_signal(barrier, 1, device_id=dest, device_id_type=MESH)

    def greet_column(i, _):
        greet({"batch": column_at(i)})
        return 0

    def greet_plane(i, _):
        greet({"batch": z * PLANE + lax.rem(j + i, PLANE)})
        return 0

    lax.fori_loop(0, n_z - 1, greet_column, 0)
    greet({"tower": tower_at(1)})
    greet({"tower": tower_at(n_tower - 1)})

    @pl.when(core == 0)
    def _():
        greet({"batch": batch_at(3)})
        greet({"batch": batch_at(-1)})

    @pl.when(core == 1)
    def _():
        greet({"batch": relay_from})
        for d in (-3, 1, 2, -2):
            greet({"batch": batch_at(d)})

    lax.fori_loop(1, PLANE, greet_plane, 0)

    loads[0].wait()
    wide = texts_ref[...].astype(jnp.float32)
    cand[0] = (wide * row_inv(wide)).astype(jnp.bfloat16)

    pl.semaphore_wait(barrier, n_z - 1 + PLANE - 1 + 2 + 3 + core)

    def cand_copy(source, target, dest, sem):
        return remote(
            cand.at[source], cand.at[target], cand_sent.at[sem], cand_here.at[target], {"batch": dest}
        )

    outward = cand_copy(0, 3 - 2 * (1 - core), batch_at(-1 - 2 * core), 0)
    to_sibling = cand_copy(0, 1, sibling, 1)
    to_relay = cand_copy(0, 4, relay_to, 1)
    pass_far = cand_copy(4, 3, relayed, 2)
    pass_near = cand_copy(3 - 2 * core, 2, sibling, 3)

    @pl.when(core == 0)
    def _():
        to_relay.start()

    outward.start()

    @pl.when(core == 1)
    def _():
        to_sibling.start()

    loads[1].wait()

    def norm(q, _):
        rows = pl.ds(q * quarter, quarter)
        values = images_ref[rows, :].astype(jnp.float32)
        inv = row_inv(values)
        img_inv[rows, :] = inv
        img_unit[rows, :] = (values * inv).astype(jnp.bfloat16)
        return 0

    lax.fori_loop(0, n_tower, norm, 0)

    logit_scale = jnp.exp(jnp.full((1, LANES), log_scale_ref[0], jnp.float32))
    bias = bias_ref[0]
    loss_acc[...] = jnp.zeros_like(loss_acc)
    diagonal = lax.broadcasted_iota(jnp.int32, (quarter, quarter), 0) == lax.broadcasted_iota(
        jnp.int32, (quarter, quarter), 1
    )

    def pairs(k, own):
        dots[...] = mxu(img_unit[...], cand[k], NT)

        def some(q, _):
            rows = pl.ds(pl.multiple_of(q * quarter, quarter), quarter)
            logits = logit_scale * dots[rows, :] + bias
            small = jnp.exp(-jnp.abs(logits))
            share = 1.0 / (1.0 + small)
            sigmoid = jnp.where(logits >= 0.0, share, small * share)
            loss = jnp.maximum(logits, 0.0) + jnp.log1p(small)
            chosen = mask_ref[q // 2, 2 * k + tower // 2].astype(jnp.float32)
            if own:
                positive = jnp.where(diagonal & (q == tower), 1.0, 0.0)
                loss = loss - positive * logits
                sigmoid = sigmoid - positive
            loss_acc[...] += chosen * loss
            cols = pl.ds(pl.multiple_of(k * quarter, quarter), quarter)
            coeffs[rows, cols] = (chosen * logit_scale * sigmoid).astype(jnp.bfloat16)
            return 0

        lax.fori_loop(0, n_tower, some, 0)

    def text_part(k):
        cols = pl.ds(pl.multiple_of(k * quarter, quarter), quarter)
        return mxu(coeffs[:, cols], img_unit[...], TN)

    def fields(values, rows):
        out = jnp.zeros((rows, LANES), jnp.int32)
        for n, value in enumerate(values):
            out = jnp.where(lane_ids(rows) == n, value, out)
        return out

    def put_rows(ref, rows, more):
        codes, power = as_codes(rows)
        for n, word in enumerate(words_of(codes, fields([power, *more], rows.shape[0]))):
            ref[:, LANES * n : LANES * (n + 1)] = word

    def get_rows(ref):
        words = [ref[:, LANES * n : LANES * (n + 1)] for n in range(5)]
        codes = [high_of(w) for w in words[1:]] + [low_of(w) for w in words[1:]] + [high_of(words[0])]
        step = step_of(low_of(words[0])[:, 0:1])
        return jnp.concatenate(codes, axis=1).astype(jnp.float32) * step

    pairs(0, True)
    own_text[...] = text_part(0)

    @pl.when(core == 0)
    def _():
        cand_copy(0, 4, me, 0).wait_recv()
        pass_far.start()

    cand_copy(0, 1, me, 0).wait_recv()

    @pl.when(core == 1)
    def _():
        pass_near.start()

    pairs(1, False)

    def core_copy(n):
        return remote(
            core_send.at[n], core_recv.at[n], core_sent.at[n], core_here.at[n], {"batch": sibling}
        )

    @pl.when(core == 0)
    def _():
        core_send[0] = text_part(1)
        core_copy(0).start()

    second_slot = 3 - core
    third_slot = 2 + core
    cand_copy(0, second_slot, me, 0).wait_recv()

    @pl.when(core == 0)
    def _():
        pass_near.start()

    pairs(second_slot, False)
    cand_copy(0, third_slot, me, 0).wait_recv()
    pairs(third_slot, False)

    total = jnp.sum(jnp.sum(loss_acc[...], axis=1, keepdims=True), axis=0, keepdims=True)

    def image_part(q):
        rows = pl.ds(pl.multiple_of(q * quarter, quarter), quarter)
        texts = cand[0:4].reshape(4 * quarter, width)
        back = mxu(coeffs[rows, :], texts, NN)
        inv = img_inv[rows, :]
        unit = images_ref[rows, :].astype(jnp.float32) * inv
        return (back - unit * jnp.sum(unit * back, axis=-1, keepdims=True)) * inv

    def cut(part):
        first, last = SUM_PARTS[part]
        return pl.ds(first * LANES, (last - first) * LANES)

    def hop_copy(part, way):
        return remote(
            tower_send.at[1, pl.ds(way * half, half), cut(part)],
            tower_relay.at[way, :, cut(part)],
            hop_sent.at[part, way],
            hop_here.at[part, way],
            {"tower": tower_at(1 + 2 * way)},
        )

    def near_copy(part, way):
        return remote(
            tower_send.at[2 * way, :, cut(part)],
            tower_recv.at[2 * way, :, cut(part)],
            near_sent.at[part, way],
            near_here.at[part, way],
            {"tower": tower_at(1 + 2 * way)},
        )

    def far_copy(part, way):
        return remote(
            tower_relay.at[way, :, cut(part)],
            tower_recv.at[1, pl.ds(way * half, half), cut(part)],
            far_sent.at[part, way],
            far_here.at[part, way],
            {"tower": tower_at(1 + 2 * way)},
        )

    def start_both(copy, part):
        if part < len(SUM_PARTS):
            for way in (0, 1):
                copy(part, way).start()

    loss_parts = loss_fields(total)
    put_rows(tower_send.at[1], image_part(tower_at(2)), loss_parts)
    start_both(hop_copy, 0)
    for way in (0, 1):
        put_rows(tower_send.at[2 * way], image_part(tower_at(1 + 2 * way)), loss_parts)
        near_copy(0, way).start()
    start_both(hop_copy, 1)

    def part_copy(n, dest):
        return remote(
            part_send.at[n], part_recv.at[n], part_sent.at[n], part_here.at[n], {"batch": dest}
        )

    far_part = part_copy(0, batch_at(2))
    near_part = part_copy(1, batch_at(3 - 2 * core))

    @pl.when(core == 1)
    def _():
        put_rows(part_send.at[0], text_part(3), [])
        far_part.start()

    core_send[1] = text_part(2)
    core_copy(1).start()
    own_image[...] = image_part(tower)

    order = order_ref
    loads[2].wait()
    place = lax.broadcasted_iota(jnp.int32, (quarter, quarter), 0)
    goal = lax.rem(z + z_step(lax.rem(place, n_z)), n_z) * PLANE + place // n_z
    picks = goal == order[...] // (n_tower * quarter)
    slots = jnp.sum(jnp.where(picks, lax.rem(order[...], quarter), 0), axis=1, keepdims=True)
    one_hot = jnp.where(picks, 1.0, 0.0).astype(jnp.bfloat16)

    def bytes_of(whole):
        return whole.astype(jnp.float32).astype(jnp.bfloat16)

    def moved(matrix, whole, dims):
        high, low = bytes_of(whole >> 8), bytes_of(whole & 0xFF)
        return mxu(matrix, high, dims) * 256.0 + mxu(matrix, low, dims)

    count = mask_ref[0, 0] * 0
    for p in range(mask_ref.shape[0]):
        for c in range(mask_ref.shape[1]):
            count = count + mask_ref[p, c]

    def plane_copy(part, peer):
        first, last = ROW_PARTS[part]
        return remote(
            row_send.at[pl.ds(first, last - first), peer],
            row_mid.at[pl.ds(first, last - first), j],
            plane_sent,
            plane_here.at[part],
            {"batch": z * PLANE + peer},
        )

    def column_copy(part, i):
        first, last = ROW_PARTS[part]
        here = row_mid.at[pl.ds(first, last - first), :, pl.ds(i, 1), :]
        there = row_recv.at[pl.ds(first, last - first), :, pl.ds(i, 1), :]
        return remote(here, there, row_sent, row_here, {"batch": column_at(i)})

    def to_plane(part):
        first, last = ROW_PARTS[part]

        def some(i, _):
            plane_copy(part, lax.rem(j + i, PLANE)).start()
            return 0

        lax.fori_loop(1, PLANE, some, 0)
        for n in range(first, last):
            row_mid[n, pl.ds(j, 1)] = row_send[n, pl.ds(j, 1)]

    def to_column(part):
        first, last = ROW_PARTS[part]
        others = row_mid.at[pl.ds(first, last - first), pl.ds(0, PLANE - 1)]
        pltpu.make_async_copy(others, others, plane_here.at[part]).wait()

        def some(i, _):
            column_copy(part, i).start()
            return 0

        lax.fori_loop(0, n_z - 1, some, 0)

    def text_sums(which):
        @pl.when(core == which)
        def _():
            core_copy(1).wait_recv()
            rest = text_part(3 - 2 * which) + core_recv[1]
            if which == 1:
                far_part.wait_recv()
                rest = rest + get_rows(part_recv.at[0])
            put_rows(part_send.at[1], rest, [])
            near_part.start()

    def pass_on(part):
        if part < len(SUM_PARTS):
            for way in (0, 1):
                hop_copy(part, way).wait_recv()
                far_copy(part, way).start()
        start_both(near_copy, part + 1)
        start_both(hop_copy, part + 2)

    powers = []
    steps = []
    spare = None
    for part, (first, last) in enumerate(SUM_PARTS):
        if part == 0:
            pass_on(0)
            text_sums(0)
            pass_on(1)
        for way in (0, 1):
            near_copy(part, way).wait_recv()
            far_copy(part, way).wait_recv()
        if part == 0:
            for n in range(3):
                extras = low_of(tower_recv[n, :, 0:LANES])
                steps.append(step_of(extras[:, 0:1]))
                total = total + loss_from(extras[0:1, 1:2], extras[0:1, 2:3], extras[0:1, 3:4])
            spare = own_image[:, 8 * LANES :]
            for n in range(3):
                spare = spare + high_of(tower_recv[n, :, 0:LANES]).astype(jnp.float32) * steps[n]
        rows = []
        for group in range(max(first, 1), last):
            high = own_image[:, (group - 1) * LANES : group * LANES]
            low = own_image[:, (group + 3) * LANES : (group + 4) * LANES]
            for n in range(3):
                word = tower_recv[n, :, group * LANES : (group + 1) * LANES]
                high = high + high_of(word).astype(jnp.float32) * steps[n]
                low = low + low_of(word).astype(jnp.float32) * steps[n]
            rows += [high, low]
        final = part == len(SUM_PARTS) - 1
        if final:
            rows.append(spare)
        codes, power = as_codes(jnp.concatenate(rows, axis=1))
        powers.append(power)
        if final:
            codes = jnp.concatenate([codes, fields(powers, quarter)], axis=1)
        codes = moved(one_hot, codes, NN).astype(jnp.int32)
        groups = [codes[:, LANES * n : LANES * (n + 1)] for n in range(codes.shape[1] // LANES)]
        if final:
            for n, value in enumerate([slots, count, *loss_fields(total)]):
                groups[-1] = jnp.where(lane_ids(quarter) == len(powers) + n, value, groups[-1])
        for n in range(len(groups) // 2):
            word = word_of(groups[2 * n], groups[2 * n + 1])
            row_send[ROW_PARTS[part][0] + n] = word.reshape(PLANE, n_z, LANES)
        to_plane(part)
        pass_on(part + 2)
        if part == 0:
            text_sums(1)
        to_column(part)

    own_here = row_mid.at[:, :, pl.ds(n_z - 1, 1), :]
    own_there = row_recv.at[:, :, pl.ds(n_z - 1, 1), :]
    own_copy = pltpu.make_async_copy(own_here, own_there, row_own)
    own_copy.start()

    near_part.wait_recv()
    own_text[...] += get_rows(part_recv.at[1])

    @pl.when(core == 1)
    def _():
        core_copy(0).wait_recv()
        own_text[...] += core_recv[0]

    back = own_text[...]
    wide = texts_ref[...].astype(jnp.float32)
    inv = row_inv(wide)
    unit = wide * inv
    text_grad_ref[...] = (back - unit * jnp.sum(unit * back, axis=-1, keepdims=True)) * inv

    own_copy.wait()
    all_rows = row_recv.at[:, :, pl.ds(0, n_z - 1), :]
    pltpu.make_async_copy(all_rows, all_rows, row_here).wait()
    words = [row_recv[n].reshape(quarter, LANES) for n in range(5)]
    extras = low_of(words[4])
    n_powers = len(powers)
    places = jnp.where(lane_ids(quarter) == extras[:, n_powers : n_powers + 1], 1.0, 0.0)
    places = places.astype(jnp.bfloat16)
    sizes = jnp.exp(moved(places, extras, TN) * LOG_STEP) * (1.0 / TOP)

    def put_group(group, whole, part):
        image_grad_ref[:, LANES * group : LANES * (group + 1)] = (
            moved(places, whole, TN) * sizes[:, part : part + 1]
        )

    for part, (first, last) in enumerate(ROW_PARTS):
        for n in range(first, min(last, 4)):
            put_group(n, high_of(words[n]), part)
            put_group(n + 4, low_of(words[n]), part)
    put_group(8, high_of(words[4]), len(ROW_PARTS) - 1)
    tail = [extras[:, n_powers + n : n_powers + n + 1] for n in range(1, 5)]
    losses = jnp.sum(loss_from(*tail[1:]), axis=0, keepdims=True)
    counts = jnp.sum(tail[0].astype(jnp.float32), axis=0, keepdims=True)
    loss_ref[...] = losses / (counts * float(4 * quarter * quarter))

    outward.wait_send()
    pass_near.wait_send()

    @pl.when(core == 0)
    def _():
        to_relay.wait_send()
        pass_far.wait_send()
        core_copy(0).wait_send()

    @pl.when(core == 1)
    def _():
        to_sibling.wait_send()
        far_part.wait_send()

    core_copy(1).wait_send()
    near_part.wait_send()
    for part in range(len(SUM_PARTS)):
        for way in (0, 1):
            hop_copy(part, way).wait_send()
            near_copy(part, way).wait_send()
            far_copy(part, way).wait_send()
    all_sent = row_send.at[:, pl.ds(0, PLANE - 1)]
    pltpu.make_async_copy(all_sent, all_sent, plane_sent).wait()
    pltpu.make_async_copy(all_rows, all_rows, row_sent).wait()


def shards(images, texts, log_scale, bias, block_mask, data_order):
    rows_group, width = images.shape
    quarter = texts.shape[0]
    words = 5 * LANES
    n_z = quarter // PLANE
    parts = len(SUM_PARTS)
    vmem = pl.BlockSpec(memory_space=pltpu.VMEM)
    smem = pl.BlockSpec(memory_space=pltpu.SMEM)
    hbm = pl.BlockSpec(memory_space=pl.ANY)
    dma = pltpu.SemaphoreType.DMA
    image_grad, text_grad, pair_loss = pl.pallas_call(
        kernel,
        out_shape=(
            jax.ShapeDtypeStruct((quarter, width), jnp.float32),
            jax.ShapeDtypeStruct((quarter, width), jnp.float32),
            jax.ShapeDtypeStruct((1, 1), jnp.float32),
        ),
        in_specs=[hbm, hbm, smem, smem, smem, hbm],
        out_specs=(vmem, vmem, vmem),
        scratch_shapes=[
            pltpu.VMEM((rows_group, width), jnp.bfloat16),
            pltpu.VMEM((quarter, width), jnp.bfloat16),
            pltpu.VMEM((1, quarter), jnp.int32),
            pltpu.VMEM((rows_group, width), jnp.bfloat16),
            pltpu.VMEM((rows_group, 1), jnp.float32),
            pltpu.VMEM((5, quarter, width), jnp.bfloat16),
            pltpu.VMEM((rows_group, 4 * quarter), jnp.bfloat16),
            pltpu.VMEM((rows_group, quarter), jnp.float32),
            pltpu.VMEM((quarter, quarter), jnp.float32),
            pltpu.VMEM((quarter, width), jnp.float32),
            pltpu.VMEM((quarter, width), jnp.float32),
            pltpu.VMEM((2, quarter, width), jnp.float32),
            pltpu.VMEM((2, quarter, width), jnp.float32),
            pltpu.VMEM((2, quarter, words), jnp.int32),
            pltpu.VMEM((2, quarter, words), jnp.int32),
            pltpu.VMEM((3, quarter, words), jnp.int32),
            pltpu.VMEM((3, quarter, words), jnp.int32),
            pltpu.VMEM((2, quarter // 2, words), jnp.int32),
            pltpu.VMEM((5, PLANE, n_z, LANES), jnp.int32),
            pltpu.VMEM((5, PLANE, n_z, LANES), jnp.int32),
            pltpu.VMEM((5, PLANE, n_z, LANES), jnp.int32),
            dma((3,)),
            dma((4,)),
            dma((5,)),
            dma((2,)),
            dma((2,)),
            dma((2,)),
            dma((2,)),
            dma((parts, 2)),
            dma((parts, 2)),
            dma((parts, 2)),
            dma((parts, 2)),
            dma((parts, 2)),
            dma((parts, 2)),
            dma,
            dma((parts,)),
            dma,
            dma,
            dma,
        ],
        compiler_params=pltpu.CompilerParams(
            collective_id=0, has_side_effects=True, vmem_limit_bytes=64 * 1024 * 1024
        ),
    )(
        images,
        texts,
        log_scale.reshape(1),
        bias.reshape(1),
        block_mask,
        data_order.reshape(1, quarter),
    )
    return image_grad, text_grad, pair_loss.reshape(())


def solution(mesh):
    in_specs = (
        P("batch", None),
        P(("batch", "tower"), None),
        P(),
        P(),
        P("batch", None),
        P(("batch", "tower")),
    )
    out_specs = (P(("batch", "tower"), None), P(("batch", "tower"), None), P())
    return jax.shard_map(shards, mesh=mesh, in_specs=in_specs, out_specs=out_specs, check_vma=False)
```

time: 80.6 us -> 74.3 us (0.922)
  Pallas kernels: 71.5 us -> 67.6 us
  local copies, waits for them, and re-layouts: 5.19 us -> 2.8 us
    pallas_call x1, Pallas kernels: 71.5 us -> 67.6 us  [shards(): pl.pallas_call(kernel, out_shape=(jax.ShapeDtypeStruct((quarter, width),...]
    unnamed x10 -> x4, local copies, waits for them, and re-layouts: 5.19 us -> 2.8 us
where the time goes in v2:
time: 74.3 us; the launch traced here: 74.1 us
  Pallas kernels  67.6 us (91%)
  between operations  3.67 us (5%)
  local copies, waits for them, and re-layouts  2.8 us (4%)
    pallas_call x1, Pallas kernels, shards(): pl.pallas_call(kernel, out_shape=(jax.ShapeDtypeStruct((quarter, width),...  67.6 us
    unnamed x4, local copies, waits for them, and re-layouts  2.8 us

profile of v2, /device:TPU:1, one launch (start us, length us, event | category | flops | bytes accessed | tf_op | source)
XLA Modules:
  0.0 74.1 jit_solution(8775840627232861620)
XLA Ops:
  1.9 67.6 %shard_map.85 = (f32[128,1152]{1,0:T(8,128)}, f32[128,1152]{1,0:T(8,128)}, f32[1,1]{1,0:T(1,128)}) custom-call(bf16[512,1152]{1,0:T(8,128)(2,1)} %images_hbm.1, bf16[128,1152]{1,0:T(8,128)(2,1)} %texts_hbm.1, f32[1]{0:T(128)} %bitcast.4.log_scale_ref, f32[1]{0:T(128)} %bitcast.5.bias_ref, s32[2,8]{1,0:T(2,128)} %mask_ref.1, s32[1,128]{1,0:T(1,128)} %bitcast.6), custom_call_target="tpu_custom_call" | custom-call | tf_op jit(solution)/shard_map/pallas_call | solution.py:611
  69.6 0.0 copy-start
  69.6 2.0 %copy.14 = f32[128,1152]{1,0:T(8,128)} copy(f32[128,1152]{1,0:T(8,128)} %get-tuple-element.12) | data formatting | bytes 1179648
  71.5 0.0 copy-done
  71.5 0.8 %copy.15 = f32[128,1152]{1,0:T(8,128)} copy(f32[128,1152]{1,0:T(8,128)S(1)} %copy-done) | data formatting | bytes 1179648
Async XLA Ops:
  69.6 2.0 %copy-start = (f32[128,1152]{1,0:T(8,128)S(1)}, f32[128,1152]{1,0:T(8,128)}, u32[]{:S(2)}) copy-start(f32[128,1152]{1,0:T(8,128)} %get-tuple-element.13) | copy-start | bytes 1769476

commit v3 on v2

--- a/solution.py
+++ b/solution.py
@@ -72,8 +72,9 @@
 
 
 PLANE = 8
-SUM_PARTS = ((0, 2), (2, 3), (3, 4), (4, 5))
-ROW_PARTS = ((0, 1), (1, 2), (2, 3), (3, 5))
+SUM_PARTS = ((0, 3), (3, 5))
+ROW_PARTS = ((0, 2), (2, 5))
+PIECES = 2
 
 
 def kernel(
@@ -103,7 +104,9 @@
     part_recv,
     tower_send,
     tower_recv,
-    tower_relay,
+    hop_send,
+    hop_recv,
+    kept,
     row_send,
     row_mid,
     row_recv,
@@ -116,10 +119,8 @@
     part_here,
     hop_sent,
     hop_here,
-    near_sent,
-    near_here,
-    far_sent,
-    far_here,
+    block_sent,
+    block_here,
     plane_sent,
     plane_here,
     row_sent,
@@ -210,26 +211,48 @@
 
     pl.semaphore_wait(barrier, n_z - 1 + PLANE - 1 + 2 + 3 + core)
 
-    def cand_copy(source, target, dest, sem):
+    piece = quarter // PIECES
+
+    def cand_copy(source, target, dest, sem, n):
+        rows = pl.ds(n * piece, piece)
         return remote(
-            cand.at[source], cand.at[target], cand_sent.at[sem], cand_here.at[target], {"batch": dest}
+            cand.at[source, rows],
+            cand.at[target, rows],
+            cand_sent.at[sem, n],
+            cand_here.at[target, n],
+            {"batch": dest},
         )
 
-    outward = cand_copy(0, 3 - 2 * (1 - core), batch_at(-1 - 2 * core), 0)
-    to_sibling = cand_copy(0, 1, sibling, 1)
-    to_relay = cand_copy(0, 4, relay_to, 1)
-    pass_far = cand_copy(4, 3, relayed, 2)
-    pass_near = cand_copy(3 - 2 * core, 2, sibling, 3)
-
-    @pl.when(core == 0)
-    def _():
-        to_relay.start()
-
-    outward.start()
+    def outward(n):
+        return cand_copy(0, 1 + 2 * core, batch_at(-1 - 2 * core), 0, n)
+
+    def to_sibling(n):
+        return cand_copy(0, 1, sibling, 1, n)
+
+    def to_relay(n):
+        return cand_copy(0, 4, relay_to, 1, n)
+
+    def pass_far(n):
+        return cand_copy(4, 3, relayed, 2, n)
+
+    def pass_near(n):
+        return cand_copy(3 - 2 * core, 2, sibling, 3, n)
+
+    def text_here(slot, n):
+        cand_copy(0, slot, me, 0, n).wait_recv()
+
+    for n in range(PIECES):
+
+        @pl.when(core == 0)
+        def _():
+            to_relay(n).start()
+
+        outward(n).start()
 
     @pl.when(core == 1)
     def _():
-        to_sibling.start()
+        for n in range(PIECES):
+            to_sibling(n).start()
 
     loads[1].wait()
 
@@ -298,14 +321,16 @@
 
     @pl.when(core == 0)
     def _():
-        cand_copy(0, 4, me, 0).wait_recv()
-        pass_far.start()
-
-    cand_copy(0, 1, me, 0).wait_recv()
-
-    @pl.when(core == 1)
-    def _():
-        pass_near.start()
+        for n in range(PIECES):
+            text_here(4, n)
+            pass_far(n).start()
+
+    for n in range(PIECES):
+        text_here(1, n)
+
+        @pl.when(core == 1)
+        def _():
+            pass_near(n).start()
 
     pairs(1, False)
 
@@ -321,69 +346,23 @@
 
     second_slot = 3 - core
     third_slot = 2 + core
-    cand_copy(0, second_slot, me, 0).wait_recv()
-
-    @pl.when(core == 0)
-    def _():
-        pass_near.start()
+    for n in range(PIECES):
+        text_here(second_slot, n)
+
+        @pl.when(core == 0)
+        def _():
+            pass_near(n).start()
 
     pairs(second_slot, False)
-    cand_copy(0, third_slot, me, 0).wait_recv()
+
+    @pl.when(core == 1)
+    def _():
+        core_send[1] = text_part(2)
+        core_copy(1).start()
+
+    for n in range(PIECES):
+        text_here(third_slot, n)
     pairs(third_slot, False)
-
-    total = jnp.sum(jnp.sum(loss_acc[...], axis=1, keepdims=True), axis=0, keepdims=True)
-
-    def image_part(q):
-        rows = pl.ds(pl.multiple_of(q * quarter, quarter), quarter)
-        texts = cand[0:4].reshape(4 * quarter, width)
-        back = mxu(coeffs[rows, :], texts, NN)
-        inv = img_inv[rows, :]
-        unit = images_ref[rows, :].astype(jnp.float32) * inv
-        return (back - unit * jnp.sum(unit * back, axis=-1, keepdims=True)) * inv
-
-    def cut(part):
-        first, last = SUM_PARTS[part]
-        return pl.ds(first * LANES, (last - first) * LANES)
-
-    def hop_copy(part, way):
-        return remote(
-            tower_send.at[1, pl.ds(way * half, half), cut(part)],
-            tower_relay.at[way, :, cut(part)],
-            hop_sent.at[part, way],
-            hop_here.at[part, way],
-            {"tower": tower_at(1 + 2 * way)},
-        )
-
-    def near_copy(part, way):
-        return remote(
-            tower_send.at[2 * way, :, cut(part)],
-            tower_recv.at[2 * way, :, cut(part)],
-            near_sent.at[part, way],
-            near_here.at[part, way],
-            {"tower": tower_at(1 + 2 * way)},
-        )
-
-    def far_copy(part, way):
-        return remote(
-            tower_relay.at[way, :, cut(part)],
-            tower_recv.at[1, pl.ds(way * half, half), cut(part)],
-            far_sent.at[part, way],
-            far_here.at[part, way],
-            {"tower": tower_at(1 + 2 * way)},
-        )
-
-    def start_both(copy, part):
-        if part < len(SUM_PARTS):
-            for way in (0, 1):
-                copy(part, way).start()
-
-    loss_parts = loss_fields(total)
-    put_rows(tower_send.at[1], image_part(tower_at(2)), loss_parts)
-    start_both(hop_copy, 0)
-    for way in (0, 1):
-        put_rows(tower_send.at[2 * way], image_part(tower_at(1 + 2 * way)), loss_parts)
-        near_copy(0, way).start()
-    start_both(hop_copy, 1)
 
     def part_copy(n, dest):
         return remote(
@@ -392,73 +371,6 @@
 
     far_part = part_copy(0, batch_at(2))
     near_part = part_copy(1, batch_at(3 - 2 * core))
-
-    @pl.when(core == 1)
-    def _():
-        put_rows(part_send.at[0], text_part(3), [])
-        far_part.start()
-
-    core_send[1] = text_part(2)
-    core_copy(1).start()
-    own_image[...] = image_part(tower)
-
-    order = order_ref
-    loads[2].wait()
-    place = lax.broadcasted_iota(jnp.int32, (quarter, quarter), 0)
-    goal = lax.rem(z + z_step(lax.rem(place, n_z)), n_z) * PLANE + place // n_z
-    picks = goal == order[...] // (n_tower * quarter)
-    slots = jnp.sum(jnp.where(picks, lax.rem(order[...], quarter), 0), axis=1, keepdims=True)
-    one_hot = jnp.where(picks, 1.0, 0.0).astype(jnp.bfloat16)
-
-    def bytes_of(whole):
-        return whole.astype(jnp.float32).astype(jnp.bfloat16)
-
-    def moved(matrix, whole, dims):
-        high, low = bytes_of(whole >> 8), bytes_of(whole & 0xFF)
-        return mxu(matrix, high, dims) * 256.0 + mxu(matrix, low, dims)
-
-    count = mask_ref[0, 0] * 0
-    for p in range(mask_ref.shape[0]):
-        for c in range(mask_ref.shape[1]):
-            count = count + mask_ref[p, c]
-
-    def plane_copy(part, peer):
-        first, last = ROW_PARTS[part]
-        return remote(
-            row_send.at[pl.ds(first, last - first), peer],
-            row_mid.at[pl.ds(first, last - first), j],
-            plane_sent,
-            plane_here.at[part],
-            {"batch": z * PLANE + peer},
-        )
-
-    def column_copy(part, i):
-        first, last = ROW_PARTS[part]
-        here = row_mid.at[pl.ds(first, last - first), :, pl.ds(i, 1), :]
-        there = row_recv.at[pl.ds(first, last - first), :, pl.ds(i, 1), :]
-        return remote(here, there, row_sent, row_here, {"batch": column_at(i)})
-
-    def to_plane(part):
-        first, last = ROW_PARTS[part]
-
-        def some(i, _):
-            plane_copy(part, lax.rem(j + i, PLANE)).start()
-            return 0
-
-        lax.fori_loop(1, PLANE, some, 0)
-        for n in range(first, last):
-            row_mid[n, pl.ds(j, 1)] = row_send[n, pl.ds(j, 1)]
-
-    def to_column(part):
-        first, last = ROW_PARTS[part]
-        others = row_mid.at[pl.ds(first, last - first), pl.ds(0, PLANE - 1)]
-        pltpu.make_async_copy(others, others, plane_here.at[part]).wait()
-
-        def some(i, _):
-            column_copy(part, i).start()
-            return 0
-
-        lax.fori_loop(0, n_z - 1, some, 0)
 
     def text_sums(which):
         @pl.when(core == which)
@@ -471,38 +383,157 @@
             put_rows(part_send.at[1], rest, [])
             near_part.start()
 
-    def pass_on(part):
-        if part < len(SUM_PARTS):
+    total = jnp.sum(jnp.sum(loss_acc[...], axis=1, keepdims=True), axis=0, keepdims=True)
+
+    def image_part(q):
+        rows = pl.ds(pl.multiple_of(q * quarter, quarter), quarter)
+        texts = cand[0:4].reshape(4 * quarter, width)
+        back = mxu(coeffs[rows, :], texts, NN)
+        inv = img_inv[rows, :]
+        unit = images_ref[rows, :].astype(jnp.float32) * inv
+        return (back - unit * jnp.sum(unit * back, axis=-1, keepdims=True)) * inv
+
+    def cut(part):
+        first, last = SUM_PARTS[part]
+        return pl.ds(first * LANES, (last - first) * LANES)
+
+    def hop_copy(way):
+        return remote(
+            hop_send.at[pl.ds(way * half, half)],
+            hop_recv.at[way],
+            hop_sent.at[way],
+            hop_here.at[way],
+            {"tower": tower_at(1 + 2 * way)},
+        )
+
+    def block_copy(part, way, summed):
+        rows = pl.ds((way if summed else 1 - way) * half, half)
+        return remote(
+            tower_send.at[way, rows, cut(part)],
+            tower_recv.at[way, rows, cut(part)],
+            block_sent.at[part, way, summed],
+            block_here.at[part, way, summed],
+            {"tower": tower_at(1 + 2 * way)},
+        )
+
+    put_rows(hop_send, image_part(tower_at(2)), loss_fields(total))
+    for way in (0, 1):
+        hop_copy(way).start()
+
+    @pl.when(core == 1)
+    def _():
+        put_rows(part_send.at[0], text_part(3), [])
+        far_part.start()
+
+    @pl.when(core == 0)
+    def _():
+        core_send[1] = text_part(2)
+        core_copy(1).start()
+
+    text_sums(0)
+
+    for way in (0, 1):
+        block = image_part(tower_at(1 + 2 * way))
+        kept[way] = block[way * half : (way + 1) * half]
+        direct = block[(1 - way) * half : (2 - way) * half]
+        put_rows(tower_send.at[way, pl.ds((1 - way) * half, half)], direct, loss_fields(total))
+        block_copy(0, way, 0).start()
+
+    own_image[...] = image_part(tower)
+
+    order = order_ref
+    loads[2].wait()
+    place = lax.broadcasted_iota(jnp.int32, (quarter, quarter), 0)
+    goal = lax.rem(z + z_step(lax.rem(place, n_z)), n_z) * PLANE + place // n_z
+    picks = goal == order[...] // (n_tower * quarter)
+    slots = jnp.sum(jnp.where(picks, lax.rem(order[...], quarter), 0), axis=1, keepdims=True)
+    one_hot = jnp.where(picks, 1.0, 0.0).astype(jnp.bfloat16)
+
+    def bytes_of(whole):
+        return whole.astype(jnp.float32).astype(jnp.bfloat16)
+
+    def moved(matrix, whole, dims):
+        high, low = bytes_of(whole >> 8), bytes_of(whole & 0xFF)
+        return mxu(matrix, high, dims) * 256.0 + mxu(matrix, low, dims)
+
+    count = mask_ref[0, 0] * 0
+    for p in range(mask_ref.shape[0]):
+        for c in range(mask_ref.shape[1]):
+            count = count + mask_ref[p, c]
+
+    def plane_copy(part, peer):
+        first, last = ROW_PARTS[part]
+        return remote(
+            row_send.at[pl.ds(first, last - first), peer],
+            row_mid.at[pl.ds(first, last - first), j],
+            plane_sent,
+            plane_here.at[part],
+            {"batch": z * PLANE + peer},
+        )
+
+    def column_copy(part, i):
+        first, last = ROW_PARTS[part]
+        here = row_mid.at[pl.ds(first, last - first), :, pl.ds(i, 1), :]
+        there = row_recv.at[pl.ds(first, last - first), :, pl.ds(i, 1), :]
+        return remote(here, there, row_sent, row_here, {"batch": column_at(i)})
+
+    def to_plane(part):
+        first, last = ROW_PARTS[part]
+
+        def some(i, _):
+            plane_copy(part, lax.rem(j + i, PLANE)).start()
+            return 0
+
+        lax.fori_loop(1, PLANE, some, 0)
+        for n in range(first, last):
+            row_mid[n, pl.ds(j, 1)] = row_send[n, pl.ds(j, 1)]
+
+    def to_column(part):
+        first, last = ROW_PARTS[part]
+        others = row_mid.at[pl.ds(first, last - first), pl.ds(0, PLANE - 1)]
+        pltpu.make_async_copy(others, others, plane_here.at[part]).wait()
+
+        def some(i, _):
+            column_copy(part, i).start()
+            return 0
+
+        lax.fori_loop(0, n_z - 1, some, 0)
+
+    def pass_on():
+        for way in (0, 1):
+            hop_copy(way).wait_recv()
+            extras = low_of(hop_recv[way, 0:8, 0:LANES])
+            both = total + loss_from(extras[0:1, 1:2], extras[0:1, 2:3], extras[0:1, 3:4])
+            rows = kept[way] + get_rows(hop_recv.at[way])
+            put_rows(tower_send.at[way, pl.ds(way * half, half)], rows, loss_fields(both))
+            block_copy(0, way, 1).start()
+        for part in range(1, len(SUM_PARTS)):
             for way in (0, 1):
-                hop_copy(part, way).wait_recv()
-                far_copy(part, way).start()
-        start_both(near_copy, part + 1)
-        start_both(hop_copy, part + 2)
+                block_copy(part, way, 0).start()
+                block_copy(part, way, 1).start()
 
     powers = []
     steps = []
     spare = None
     for part, (first, last) in enumerate(SUM_PARTS):
         if part == 0:
-            pass_on(0)
-            text_sums(0)
-            pass_on(1)
+            pass_on()
         for way in (0, 1):
-            near_copy(part, way).wait_recv()
-            far_copy(part, way).wait_recv()
+            for summed in (0, 1):
+                block_copy(part, way, summed).wait_recv()
         if part == 0:
-            for n in range(3):
+            for n in range(2):
                 extras = low_of(tower_recv[n, :, 0:LANES])
                 steps.append(step_of(extras[:, 0:1]))
                 total = total + loss_from(extras[0:1, 1:2], extras[0:1, 2:3], extras[0:1, 3:4])
             spare = own_image[:, 8 * LANES :]
-            for n in range(3):
+            for n in range(2):
                 spare = spare + high_of(tower_recv[n, :, 0:LANES]).astype(jnp.float32) * steps[n]
         rows = []
         for group in range(max(first, 1), last):
             high = own_image[:, (group - 1) * LANES : group * LANES]
             low = own_image[:, (group + 3) * LANES : (group + 4) * LANES]
-            for n in range(3):
+            for n in range(2):
                 word = tower_recv[n, :, group * LANES : (group + 1) * LANES]
                 high = high + high_of(word).astype(jnp.float32) * steps[n]
                 low = low + low_of(word).astype(jnp.float32) * steps[n]
@@ -523,7 +554,6 @@
             word = word_of(groups[2 * n], groups[2 * n + 1])
             row_send[ROW_PARTS[part][0] + n] = word.reshape(PLANE, n_z, LANES)
         to_plane(part)
-        pass_on(part + 2)
         if part == 0:
             text_sums(1)
         to_column(part)
@@ -572,30 +602,51 @@
     counts = jnp.sum(tail[0].astype(jnp.float32), axis=0, keepdims=True)
     loss_ref[...] = losses / (counts * float(4 * quarter * quarter))
 
-    outward.wait_send()
-    pass_near.wait_send()
+    for n in range(PIECES):
+        outward(n).wait_send()
+        pass_near(n).wait_send()
 
     @pl.when(core == 0)
     def _():
-        to_relay.wait_send()
-        pass_far.wait_send()
+        for n in range(PIECES):
+            to_relay(n).wait_send()
+            pass_far(n).wait_send()
         core_copy(0).wait_send()
 
     @pl.when(core == 1)
     def _():
-        to_sibling.wait_send()
+        for n in range(PIECES):
+            to_sibling(n).wait_send()
         far_part.wait_send()
 
     core_copy(1).wait_send()
     near_part.wait_send()
-    for part in range(len(SUM_PARTS)):
-        for way in (0, 1):
-            hop_copy(part, way).wait_send()
-            near_copy(part, way).wait_send()
-            far_copy(part, way).wait_send()
+    for way in (0, 1):
+        hop_copy(way).wait_send()
+        for part in range(len(SUM_PARTS)):
+            for summed in (0, 1):
+                block_copy(part, way, summed).wait_send()
     all_sent = row_send.at[:, pl.ds(0, PLANE - 1)]
     pltpu.make_async_copy(all_sent, all_sent, plane_sent).wait()
     pltpu.make_async_copy(all_rows, all_rows, row_sent).wait()
+
+
+def hand_out(image_in, text_in, image_out, text_out, held, done):
+    ins = [
+        pltpu.make_async_copy(image_in, held.at[0], done.at[0]),
+        pltpu.make_async_copy(text_in, held.at[1], done.at[1]),
+    ]
+    outs = [
+        pltpu.make_async_copy(held.at[0], image_out, done.at[2]),
+        pltpu.make_async_copy(held.at[1], text_out, done.at[3]),
+    ]
+    for copy in ins:
+        copy.start()
+    for n in range(2):
+        ins[n].wait()
+        outs[n].start()
+    for copy in outs:
+        copy.wait()
 
 
 def shards(images, texts, log_scale, bias, block_mask, data_order):
@@ -633,25 +684,25 @@
             pltpu.VMEM((2, quarter, width), jnp.float32),
             pltpu.VMEM((2, quarter, words), jnp.int32),
             pltpu.VMEM((2, quarter, words), jnp.int32),
-            pltpu.VMEM((3, quarter, words), jnp.int32),
-            pltpu.VMEM((3, quarter, words), jnp.int32),
+            pltpu.VMEM((2, quarter, words), jnp.int32),
+            pltpu.VMEM((2, quarter, words), jnp.int32),
+            pltpu.VMEM((quarter, words), jnp.int32),
             pltpu.VMEM((2, quarter // 2, words), jnp.int32),
+            pltpu.VMEM((2, quarter // 2, width), jnp.float32),
             pltpu.VMEM((5, PLANE, n_z, LANES), jnp.int32),
             pltpu.VMEM((5, PLANE, n_z, LANES), jnp.int32),
             pltpu.VMEM((5, PLANE, n_z, LANES), jnp.int32),
             dma((3,)),
-            dma((4,)),
-            dma((5,)),
+            dma((4, PIECES)),
+            dma((5, PIECES)),
             dma((2,)),
             dma((2,)),
             dma((2,)),
             dma((2,)),
-            dma((parts, 2)),
-            dma((parts, 2)),
-            dma((parts, 2)),
-            dma((parts, 2)),
-            dma((parts, 2)),
-            dma((parts, 2)),
+            dma((2,)),
+            dma((2,)),
+            dma((parts, 2, 2)),
+            dma((parts, 2, 2)),
             dma,
             dma((parts,)),
             dma,
@@ -669,6 +720,16 @@
         block_mask,
         data_order.reshape(1, quarter),
     )
+    image_grad, text_grad = pl.pallas_call(
+        hand_out,
+        out_shape=(
+            jax.ShapeDtypeStruct((quarter, width), jnp.float32),
+            jax.ShapeDtypeStruct((quarter, width), jnp.float32),
+        ),
+        in_specs=[pl.BlockSpec(memory_space=pltpu.HBM)] * 2,
+        out_specs=(pl.BlockSpec(memory_space=pltpu.HBM),) * 2,
+        scratch_shapes=[pltpu.VMEM((2, quarter, width), jnp.float32), dma((4,))],
+    )(image_grad, text_grad)
     return image_grad, text_grad, pair_loss.reshape(())
 
 

time: 74.3 us -> 69.5 us (0.935)
  local copies, waits for them, and re-layouts: 2.8 us -> 0 us
  Pallas kernels: 67.6 us -> 65.5 us
    pallas_call x1, Pallas kernels: 67.6 us -> 63.4 us  [shards(): pl.pallas_call(kernel, out_shape=(jax.ShapeDtypeStruct((quarter, width),...]
    unnamed x4 -> x0, local copies, waits for them, and re-layouts: 2.8 us -> none
    pallas_call x0 -> x1, Pallas kernels: none -> 2.11 us  [shards(): pl.pallas_call(hand_out, out_shape=(jax.ShapeDtypeStruct((quarter, width)...]
where the time goes in v3:
time: 69.5 us; the launch traced here: 69.1 us
  Pallas kernels  65.5 us (94%)
  between operations  3.67 us (5%)
    pallas_call x1, Pallas kernels, shards(): pl.pallas_call(kernel, out_shape=(jax.ShapeDtypeStruct((quarter, width),...  63.4 us
    pallas_call x1, Pallas kernels, shards(): pl.pallas_call(hand_out, out_shape=(jax.ShapeDtypeStruct((quarter, width)...  2.11 us

profile of v3, /device:TPU:1, one launch (start us, length us, event | category | flops | bytes accessed | tf_op | source)
XLA Modules:
  0.0 69.1 jit_solution(18364661337257296005)
XLA Ops:
  1.9 63.4 %shard_map.85 = (f32[128,1152]{1,0:T(8,128)}, f32[128,1152]{1,0:T(8,128)}, f32[1,1]{1,0:T(1,128)}) custom-call(bf16[512,1152]{1,0:T(8,128)(2,1)} %images_hbm.1, bf16[128,1152]{1,0:T(8,128)(2,1)} %texts_hbm.1, f32[1]{0:T(128)} %bitcast.4.log_scale_ref, f32[1]{0:T(128)} %bitcast.5.bias_ref, s32[2,8]{1,0:T(2,128)} %mask_ref.1, s32[1,128]{1,0:T(1,128)} %bitcast.6), custom_call_target="tpu_custom_call" | custom-call | tf_op jit(solution)/shard_map/pallas_call | solution.py:662
  65.3 2.1 %shard_map.86 = (f32[128,1152]{1,0:T(8,128)}, f32[128,1152]{1,0:T(8,128)}) custom-call(f32[128,1152]{1,0:T(8,128)} %get-tuple-element.8.image_in, f32[128,1152]{1,0:T(8,128)} %get-tuple-element.9.text_in), custom_call_target="tpu_custom_call" | custom-call | tf_op jit(solution)/shard_map/pallas_call | solution.py:723

commit v4 on v3

--- a/solution.py
+++ b/solution.py
@@ -58,6 +58,15 @@
     return (word << 16) >> 16
 
 
+def bytes_of(whole):
+    return whole.astype(jnp.float32).astype(jnp.bfloat16)
+
+
+def moved(matrix, whole, dims):
+    high, low = bytes_of(whole >> 8), bytes_of(whole & 0xFF)
+    return mxu(matrix, high, dims) * 256.0 + mxu(matrix, low, dims)
+
+
 def loss_fields(total):
     power = jnp.ceil(jnp.log(jnp.maximum(total, 1e-30)) * (1.0 / 0.6931471805599453))
     scaled = total * jnp.exp(power * -0.6931471805599453) * 8192.0
@@ -84,8 +93,8 @@
     bias_ref,
     mask_ref,
     order_hbm,
-    image_grad_ref,
-    text_grad_ref,
+    words_hbm,
+    text_hbm,
     loss_ref,
     images_ref,
     texts_ref,
@@ -126,6 +135,8 @@
     row_sent,
     row_here,
     row_own,
+    text_grad_ref,
+    out_here,
 ):
     n_batch = lax.axis_size("batch")
     n_tower = lax.axis_size("tower")
@@ -449,13 +460,6 @@
     slots = jnp.sum(jnp.where(picks, lax.rem(order[...], quarter), 0), axis=1, keepdims=True)
     one_hot = jnp.where(picks, 1.0, 0.0).astype(jnp.bfloat16)
 
-    def bytes_of(whole):
-        return whole.astype(jnp.float32).astype(jnp.bfloat16)
-
-    def moved(matrix, whole, dims):
-        high, low = bytes_of(whole >> 8), bytes_of(whole & 0xFF)
-        return mxu(matrix, high, dims) * 256.0 + mxu(matrix, low, dims)
-
     count = mask_ref[0, 0] * 0
     for p in range(mask_ref.shape[0]):
         for c in range(mask_ref.shape[1]):
@@ -507,10 +511,6 @@
             rows = kept[way] + get_rows(hop_recv.at[way])
             put_rows(tower_send.at[way, pl.ds(way * half, half)], rows, loss_fields(both))
             block_copy(0, way, 1).start()
-        for part in range(1, len(SUM_PARTS)):
-            for way in (0, 1):
-                block_copy(part, way, 0).start()
-                block_copy(part, way, 1).start()
 
     powers = []
     steps = []
@@ -529,6 +529,10 @@
             spare = own_image[:, 8 * LANES :]
             for n in range(2):
                 spare = spare + high_of(tower_recv[n, :, 0:LANES]).astype(jnp.float32) * steps[n]
+        if part + 1 < len(SUM_PARTS):
+            for way in (0, 1):
+                block_copy(part + 1, way, 0).start()
+                block_copy(part + 1, way, 1).start()
         rows = []
         for group in range(max(first, 1), last):
             high = own_image[:, (group - 1) * LANES : group * LANES]
@@ -576,27 +580,16 @@
     inv = row_inv(wide)
     unit = wide * inv
     text_grad_ref[...] = (back - unit * jnp.sum(unit * back, axis=-1, keepdims=True)) * inv
+    text_out = pltpu.make_async_copy(text_grad_ref, text_hbm, out_here.at[0])
+    text_out.start()
 
     own_copy.wait()
     all_rows = row_recv.at[:, :, pl.ds(0, n_z - 1), :]
     pltpu.make_async_copy(all_rows, all_rows, row_here).wait()
-    words = [row_recv[n].reshape(quarter, LANES) for n in range(5)]
-    extras = low_of(words[4])
-    n_powers = len(powers)
-    places = jnp.where(lane_ids(quarter) == extras[:, n_powers : n_powers + 1], 1.0, 0.0)
-    places = places.astype(jnp.bfloat16)
-    sizes = jnp.exp(moved(places, extras, TN) * LOG_STEP) * (1.0 / TOP)
-
-    def put_group(group, whole, part):
-        image_grad_ref[:, LANES * group : LANES * (group + 1)] = (
-            moved(places, whole, TN) * sizes[:, part : part + 1]
-        )
-
-    for part, (first, last) in enumerate(ROW_PARTS):
-        for n in range(first, min(last, 4)):
-            put_group(n, high_of(words[n]), part)
-            put_group(n + 4, low_of(words[n]), part)
-    put_group(8, high_of(words[4]), len(ROW_PARTS) - 1)
+    words_out = pltpu.make_async_copy(row_recv, words_hbm, out_here.at[1])
+    words_out.start()
+    extras = low_of(row_recv[4]).reshape(quarter, LANES)
+    n_powers = len(ROW_PARTS)
     tail = [extras[:, n_powers + n : n_powers + n + 1] for n in range(1, 5)]
     losses = jnp.sum(loss_from(*tail[1:]), axis=0, keepdims=True)
     counts = jnp.sum(tail[0].astype(jnp.float32), axis=0, keepdims=True)
@@ -629,24 +622,41 @@
     all_sent = row_send.at[:, pl.ds(0, PLANE - 1)]
     pltpu.make_async_copy(all_sent, all_sent, plane_sent).wait()
     pltpu.make_async_copy(all_rows, all_rows, row_sent).wait()
-
-
-def hand_out(image_in, text_in, image_out, text_out, held, done):
-    ins = [
-        pltpu.make_async_copy(image_in, held.at[0], done.at[0]),
-        pltpu.make_async_copy(text_in, held.at[1], done.at[1]),
-    ]
-    outs = [
-        pltpu.make_async_copy(held.at[0], image_out, done.at[2]),
-        pltpu.make_async_copy(held.at[1], text_out, done.at[3]),
-    ]
-    for copy in ins:
-        copy.start()
-    for n in range(2):
-        ins[n].wait()
-        outs[n].start()
-    for copy in outs:
-        copy.wait()
+    text_out.wait()
+    words_out.wait()
+
+
+def hand_out(words_hbm, text_in, image_out, text_out, words_ref, text_ref, image_ref, done):
+    words_in = pltpu.make_async_copy(words_hbm, words_ref, done.at[0])
+    text_load = pltpu.make_async_copy(text_in, text_ref, done.at[1])
+    image_store = pltpu.make_async_copy(image_ref, image_out, done.at[2])
+    text_store = pltpu.make_async_copy(text_ref, text_out, done.at[3])
+    words_in.start()
+    text_load.start()
+    words_in.wait()
+    quarter = image_ref.shape[0]
+    words = [words_ref[n].reshape(quarter, LANES) for n in range(5)]
+    extras = low_of(words[4])
+    n_powers = len(ROW_PARTS)
+    places = jnp.where(lane_ids(quarter) == extras[:, n_powers : n_powers + 1], 1.0, 0.0)
+    places = places.astype(jnp.bfloat16)
+    sizes = jnp.exp(moved(places, extras, TN) * LOG_STEP) * (1.0 / TOP)
+    text_load.wait()
+    text_store.start()
+
+    def put_group(group, whole, part):
+        image_ref[:, LANES * group : LANES * (group + 1)] = (
+            moved(places, whole, TN) * sizes[:, part : part + 1]
+        )
+
+    for part, (first, last) in enumerate(ROW_PARTS):
+        for n in range(first, min(last, 4)):
+            put_group(n, high_of(words[n]), part)
+            put_group(n + 4, low_of(words[n]), part)
+    put_group(8, high_of(words[4]), len(ROW_PARTS) - 1)
+    image_store.start()
+    text_store.wait()
+    image_store.wait()
 
 
 def shards(images, texts, log_scale, bias, block_mask, data_order):
@@ -659,15 +669,15 @@
     smem = pl.BlockSpec(memory_space=pltpu.SMEM)
     hbm = pl.BlockSpec(memory_space=pl.ANY)
     dma = pltpu.SemaphoreType.DMA
-    image_grad, text_grad, pair_loss = pl.pallas_call(
+    arrived, text_grad, pair_loss = pl.pallas_call(
         kernel,
         out_shape=(
-            jax.ShapeDtypeStruct((quarter, width), jnp.float32),
+            jax.ShapeDtypeStruct((5, PLANE, n_z, LANES), jnp.int32),
             jax.ShapeDtypeStruct((quarter, width), jnp.float32),
             jax.ShapeDtypeStruct((1, 1), jnp.float32),
         ),
         in_specs=[hbm, hbm, smem, smem, smem, hbm],
-        out_specs=(vmem, vmem, vmem),
+        out_specs=(hbm, hbm, vmem),
         scratch_shapes=[
             pltpu.VMEM((rows_group, width), jnp.bfloat16),
             pltpu.VMEM((quarter, width), jnp.bfloat16),
@@ -708,6 +718,8 @@
             dma,
             dma,
             dma,
+            pltpu.VMEM((quarter, width), jnp.float32),
+            dma((2,)),
         ],
         compiler_params=pltpu.CompilerParams(
             collective_id=0, has_side_effects=True, vmem_limit_bytes=64 * 1024 * 1024
@@ -728,8 +740,14 @@
         ),
         in_specs=[pl.BlockSpec(memory_space=pltpu.HBM)] * 2,
         out_specs=(pl.BlockSpec(memory_space=pltpu.HBM),) * 2,
-        scratch_shapes=[pltpu.VMEM((2, quarter, width), jnp.float32), dma((4,))],
-    )(image_grad, text_grad)
+        scratch_shapes=[
+            pltpu.VMEM((5, PLANE, n_z, LANES), jnp.int32),
+            pltpu.VMEM((quarter, width), jnp.float32),
+            pltpu.VMEM((quarter, width), jnp.float32),
+            dma((4,)),
+        ],
+        compiler_params=pltpu.CompilerParams(vmem_limit_bytes=64 * 1024 * 1024),
+    )(arrived, text_grad)
     return image_grad, text_grad, pair_loss.reshape(())
 
 

time: 69.5 us -> 69.4 us (level)
  no operation moved by 1% of the time
where the time goes in v4:
time: 69.4 us; the launch traced here: 69.2 us
  Pallas kernels  65.5 us (94%)
  between operations  3.68 us (5%)
    pallas_call x1, Pallas kernels, shards(): pl.pallas_call(kernel, out_shape=(jax.ShapeDtypeStruct((5, PLANE, n_z, LA...  63.1 us
    pallas_call x1, Pallas kernels, shards(): pl.pallas_call(hand_out, out_shape=(jax.ShapeDtypeStruct((quarter, width)...  2.43 us

profile of v4, /device:TPU:1, one launch (start us, length us, event | category | flops | bytes accessed | tf_op | source)
XLA Modules:
  0.0 69.2 jit_solution(10321921082556368710)
XLA Ops:
  1.9 63.1 %shard_map.85 = (s32[5,8,16,128]{3,2,1,0:T(8,128)}, f32[128,1152]{1,0:T(8,128)}, f32[1,1]{1,0:T(1,128)}) custom-call(bf16[512,1152]{1,0:T(8,128)(2,1)} %images_hbm.1, bf16[128,1152]{1,0:T(8,128)(2,1)} %texts_hbm.1, f32[1]{0:T(128)} %bitcast.4.log_scale_ref, f32[1]{0:T(128)} %bitcast.5.bias_ref, s32[2,8]{1,0:T(2,128)} %mask_ref.1, s32[1,128]{1,0:T(1,128)} %bitcast.6), custom_call_target="tpu_custom_call" | custom-call | tf_op jit(solution)/shard_map/pallas_call | solution.py:672
  65.0 2.4 %shard_map.86 = (f32[128,1152]{1,0:T(8,128)}, f32[128,1152]{1,0:T(8,128)}) custom-call(s32[5,8,16,128]{3,2,1,0:T(8,128)} %get-tuple-element.8.words_hbm, f32[128,1152]{1,0:T(8,128)} %get-tuple-element.9.text_in), custom_call_target="tpu_custom_call" | custom-call | tf_op jit(solution)/shard_map/pallas_call | solution.py:735
